TPU v7x, 32 devices: a whole 2x2x4 slice. The times are simulated.
32 devices in a mesh: dp: 4 (over y, x), pipe: 8 (over z, core).
Axes of the slice: x: 2, y: 2, z: 4, core: 2. Of those that a mesh axis runs over, the one named last changes fastest.
Arguments:
- weights: bfloat16 [8, 2, 3840, 512], P('pipe'), as said below
- master: float32 [8, 3840, 512], P('pipe', 'dp')
- moment1: bfloat16 [8, 3840, 512], P('pipe', 'dp'), may hold values from -1.5 to 1.5
- moment2: bfloat16 [8, 3840, 512], P('pipe', 'dp'), may hold values from 0.0099487305 to 1
- saved: bfloat16 [8, 2, 4, 64, 3840], P('pipe', None, None, 'dp')
- cotangent: bfloat16 [2, 4, 64, 3840], P(None, None, 'dp'), may hold values from -0.75 to 0.75
Outputs:
- new_master: float32 [8, 3840, 512], P('pipe', 'dp')
- new_moment1: bfloat16 [8, 3840, 512], P('pipe', 'dp')
- new_moment2: bfloat16 [8, 3840, 512], P('pipe', 'dp')
Inputs may be any that keep to these rules, and one draw needn't show every extreme that they name: weights[i, 1] equals weights[7 - i, 0], and weights[i, 0] is master[i] rounded to bfloat16.
All inputs are finite; a program needn't handle non-finite values.
Results may differ from a plain program's by a relative error of at most 0.0075.
Values may be sent and summed in bfloat16 or wider, within the bound.
A program may use at most 128 MiB of HBM per device.

v0:
```python
import jax
import jax.numpy as jnp
from jax import lax
from jax.sharding import PartitionSpec as P

norm_epsilon = 1e-06
first_decay = 0.9
second_decay = 0.95
adam_epsilon = 1e-08
learn_rate = 0.00022
weight_decay = 0.1
step_count = 100.0


def from_behind(array, axis, by):
    count = lax.axis_size(axis)
    pairs = [(i, i + by) for i in range(count) if 0 <= i + by < count]
    return lax.ppermute(array, axis, pairs)


def from_partner(value, axis, apart):
    mask = 2**apart
    pairs = [(source, source ^ mask) for source in range(lax.axis_size(axis))]
    return lax.ppermute(value, axis, pairs)


def section_backward(inputs, grad_out, section_weights):
    latent_width = section_weights.shape[1] // 2
    down_proj = section_weights[:, :latent_width]
    up_proj = section_weights[:, latent_width:]
    values = inputs.astype(jnp.float32)
    row_scale = lax.rsqrt(jnp.mean(values * values, axis=-1, keepdims=True) + norm_epsilon)
    normed = (values * row_scale).astype(jnp.bfloat16)
    latent = jnp.dot(normed, down_proj, preferred_element_type=jnp.float32)
    latent_scale = lax.rsqrt(jnp.mean(latent * latent, axis=-1, keepdims=True) + norm_epsilon)
    latent_act = (latent * latent_scale).astype(jnp.bfloat16)
    grad_act = jnp.dot(grad_out, up_proj, preferred_element_type=jnp.float32)
    grad_latent = latent_scale * grad_act - latent * latent_scale**3 * jnp.mean(
        latent * grad_act, axis=-1, keepdims=True
    )
    grad_latent = grad_latent.astype(jnp.bfloat16)
    grad_normed = jnp.dot(grad_latent, down_proj.T, preferred_element_type=jnp.float32)
    grad_in = (
        grad_out.astype(jnp.float32)
        + row_scale * grad_normed
        - values * row_scale**3 * jnp.mean(values * grad_normed, axis=-1, keepdims=True)
    )
    return (grad_in.astype(jnp.bfloat16), normed, latent_act, grad_latent)


def adamw(master, moment1, moment2, gradient):
    first_new = first_decay * moment1.astype(jnp.float32) + (1.0 - first_decay) * gradient
    second_new = (
        second_decay * moment2.astype(jnp.float32) + (1.0 - second_decay) * gradient * gradient
    )
    first_hat = first_new / (1.0 - first_decay**step_count)
    second_hat = second_new / (1.0 - second_decay**step_count)
    updated = master - learn_rate * (
        first_hat / (jnp.sqrt(second_hat) + adam_epsilon) + weight_decay * master
    )
    return (updated, first_new.astype(jnp.bfloat16), second_new.astype(jnp.bfloat16))


def store_slot(stored, fresh, clipped, active):
    previous = lax.dynamic_index_in_dim(stored, clipped, 0, keepdims=False)
    chosen = jnp.where(active, fresh, previous)
    return lax.dynamic_update_index_in_dim(stored, chosen, clipped, 0)


def wide_rows(stash):
    output_store, normalized_store, activation_store, latent_store = stash
    return jnp.stack([normalized_store, output_store])[:, :, None]


def narrow_rows(stash):
    output_store, normalized_store, activation_store, latent_store = stash
    return jnp.stack([latent_store, activation_store])[:, :, None]


def shard_gradient(received_wide, received_narrow):
    down_part = jnp.einsum(
        "mrtd,mrtk->rdk", received_wide[0], received_narrow[0], preferred_element_type=jnp.float32
    )
    up_part = jnp.einsum(
        "mrtd,mrtk->rdk", received_wide[1], received_narrow[1], preferred_element_type=jnp.float32
    )
    rounded = jnp.concatenate([down_part, up_part], axis=2).astype(jnp.bfloat16)
    rounded = lax.optimization_barrier(rounded)
    return jnp.sum(rounded.astype(jnp.float32), axis=0)


def shards(weights, master, moment1, moment2, saved, cotangent):
    sections = lax.axis_size("pipe")
    position = lax.axis_index("pipe")
    micro_count = saved.shape[2]
    batch_rows = saved.shape[3]
    features = saved.shape[4]
    latent_width = weights.shape[3] // 2
    local_inputs = saved[0]
    local_weights = weights[0]

    def single_sense_pass(travel_sense, holder_index, has_landed, reached_final, saved_stores):
        output_store, normalized_store, activation_store, latent_store = saved_stores
        active = (holder_index >= 0) & (holder_index < micro_count)
        clipped = jnp.clip(holder_index, 0, micro_count - 1)
        entry = lax.dynamic_index_in_dim(cotangent[travel_sense], clipped, 0, keepdims=False)
        grad_out = jnp.where(reached_final, entry, has_landed)
        inputs = lax.dynamic_index_in_dim(local_inputs[travel_sense], clipped, 0, keepdims=False)

        def compute():
            return section_backward(inputs, grad_out, local_weights[travel_sense])

        def skipped():
            empty_latent = jnp.zeros((batch_rows, latent_width), jnp.bfloat16)
            empty_rows = jnp.zeros((batch_rows, features), jnp.bfloat16)
            return (empty_rows, empty_rows, empty_latent, empty_latent)

        grad_in, normed, latent_act, grad_latent = lax.cond(active, compute, skipped)
        output_store = store_slot(output_store, grad_out, clipped, active)
        normalized_store = store_slot(normalized_store, normed, clipped, active)
        activation_store = store_slot(activation_store, latent_act, clipped, active)
        latent_store = store_slot(latent_store, grad_latent, clipped, active)
        return (grad_in, (output_store, normalized_store, activation_store, latent_store))

    def advance(tick_index, carried):
        sent_down, sent_up, low_stash, high_stash = carried
        from_above = from_behind(sent_down, "pipe", -1)
        from_below = from_behind(sent_up, "pipe", 1)
        next_down, low_stash = single_sense_pass(
            0,
            tick_index - (sections - 1 - position),
            from_above,
            position == sections - 1,
            low_stash,
        )
        next_up, high_stash = single_sense_pass(
            1, tick_index - position, from_below, position == 0, high_stash
        )
        return (next_down, next_up, low_stash, high_stash)

    empty_rows = jnp.zeros((batch_rows, features), jnp.bfloat16)
    stash_rows = jnp.zeros((micro_count, batch_rows, features), jnp.bfloat16)
    stash_latent = jnp.zeros((micro_count, batch_rows, latent_width), jnp.bfloat16)
    fresh_stash = (stash_rows, stash_rows, stash_latent, stash_latent)
    carried = (empty_rows, empty_rows, fresh_stash, fresh_stash)
    tick_total = sections - 1 + micro_count
    carried = lax.fori_loop(0, tick_total, advance, carried)
    wide_both = jnp.stack([wide_rows(carried[2]), wide_rows(carried[3])])
    narrow_both = jnp.stack([narrow_rows(carried[2]), narrow_rows(carried[3])])
    wide_recv = lax.all_to_all(wide_both, "dp", split_axis=5, concat_axis=3, tiled=True)
    narrow_recv = lax.all_gather(narrow_both, "dp", axis=3, tiled=True)
    ahead_sum = shard_gradient(wide_recv[0], narrow_recv[0])
    behind_sum = shard_gradient(wide_recv[1], narrow_recv[1])
    bit_count = sections.bit_length() - 1
    bit_order = list(range(bit_count))
    partner_sum = behind_sum
    for bit_index in bit_order:
        partner_sum = from_partner(partner_sum.astype(jnp.bfloat16), "pipe", bit_index).astype(
            partner_sum.dtype
        )
    gradient = ahead_sum + partner_sum
    new_master, new_first, new_second = adamw(master[0], moment1[0], moment2[0], gradient)
    return (new_master[None], new_first[None], new_second[None])


def solution(mesh):
    return jax.shard_map(
        shards,
        mesh=mesh,
        in_specs=(
            P("pipe", None, None, None),
            P("pipe", "dp", None),
            P("pipe", "dp", None),
            P("pipe", "dp", None),
            P("pipe", None, None, "dp", None),
            P(None, None, "dp", None),
        ),
        out_specs=(P("pipe", "dp", None), P("pipe", "dp", None), P("pipe", "dp", None)),
        check_vma=False,
    )
```

profile of v0, /device:TPU:0, one launch (start us, length us, event | category | flops | bytes accessed | tf_op | source)
XLA Modules:
  0.0 526.0 jit_solution(10506019199567655171)
XLA Ops:
  6.5 321.6 %while.32 = (s32[]{:T(128)}, bf16[16,3840]{1,0:T(8,128)(2,1)}, bf16[16,3840]{1,0:T(8,128)(2,1)}, bf16[4,16,3840]{2,1,0:T(8,128)(2,1)}, bf16[4,16,3840]{2,1,0:T(8...) while((s32[]{:T(128)}, bf16[16,3840]{1,0:T(8,128)(2,1)}, ...), condition=%wide.region_13.14_spmd, body=%wide.region_0.13_spmd.sunk | while | flops 191307968 | bytes 39951116 | solution.py:147
  7.8 3.7 collective-permute-start.1
  19.4 1.9 conditional.4
  22.0 8.0 %conditional.5 = (bf16[16,3840]{1,0:T(8,128)(2,1)}, bf16[16,3840]{1,0:T(8,128)(2,1)}, bf16[16,256]{1,0:T(8,128)(2,1)S(1)}, bf16[16,256]{1,0:T(8,128)(2,1)}) conditional(s32[]{:T(128)} %convert_element_type.145, () %tuple.97, (bf16[16,3840]{1,0:T(8,128)(2,1)S(1)}, bf16[2,4,16,3840]{3,2,1,0:T(8,128)(2,1)S(1)}, s32[]{:T(128)}, ...), branch_computations={%region_7.7_spmd, %region_8.12_spmd} | conditional | flops 95461472 | bytes 16450928 | solution.py:118
  22.0 2.4 slice_bitcast_fusion.1
  34.2 3.7 collective-permute-start.1
  45.8 1.9 conditional.4
  48.5 8.0 %conditional.5 = (bf16[16,3840]{1,0:T(8,128)(2,1)}, bf16[16,3840]{1,0:T(8,128)(2,1)}, bf16[16,256]{1,0:T(8,128)(2,1)S(1)}, bf16[16,256]{1,0:T(8,128)(2,1)}) conditional(s32[]{:T(128)} %convert_element_type.145, () %tuple.97, (bf16[16,3840]{1,0:T(8,128)(2,1)S(1)}, bf16[2,4,16,3840]{3,2,1,0:T(8,128)(2,1)S(1)}, s32[]{:T(128)}, ...), branch_computations={%region_7.7_spmd, %region_8.12_spmd} | conditional | flops 95461472 | bytes 16450928 | solution.py:118
  48.5 2.4 slice_bitcast_fusion.1
  60.7 3.7 collective-permute-start.1
  72.3 1.9 conditional.4
  74.9 8.0 %conditional.5 = (bf16[16,3840]{1,0:T(8,128)(2,1)}, bf16[16,3840]{1,0:T(8,128)(2,1)}, bf16[16,256]{1,0:T(8,128)(2,1)S(1)}, bf16[16,256]{1,0:T(8,128)(2,1)}) conditional(s32[]{:T(128)} %convert_element_type.145, () %tuple.97, (bf16[16,3840]{1,0:T(8,128)(2,1)S(1)}, bf16[2,4,16,3840]{3,2,1,0:T(8,128)(2,1)S(1)}, s32[]{:T(128)}, ...), branch_computations={%region_7.7_spmd, %region_8.12_spmd} | conditional | flops 95461472 | bytes 16450928 | solution.py:118
  75.0 2.4 slice_bitcast_fusion.1
  87.2 5.0 collective-permute-start.1
  100.0 1.9 conditional.4
  102.7 8.0 %conditional.5 = (bf16[16,3840]{1,0:T(8,128)(2,1)}, bf16[16,3840]{1,0:T(8,128)(2,1)}, bf16[16,256]{1,0:T(8,128)(2,1)S(1)}, bf16[16,256]{1,0:T(8,128)(2,1)}) conditional(s32[]{:T(128)} %convert_element_type.145, () %tuple.97, (bf16[16,3840]{1,0:T(8,128)(2,1)S(1)}, bf16[2,4,16,3840]{3,2,1,0:T(8,128)(2,1)S(1)}, s32[]{:T(128)}, ...), branch_computations={%region_7.7_spmd, %region_8.12_spmd} | conditional | flops 95461472 | bytes 16450928 | solution.py:118
  102.7 2.4 slice_bitcast_fusion.1
  114.9 5.2 collective-permute-start.1
  128.0 1.9 conditional.4
  135.1 12.9 %collective-permute-start.1 = (bf16[16,3840]{1,0:T(8,128)(2,1)}, bf16[16,3840]{1,0:T(8,128)(2,1)}, u32[]{:S(2)}, u32[]{:S(2)}) collective-permute-start(bf16[16,3840]{1,0:T(8,128)(2,1)} %get-tuple-element.661), channel_id=1, source_target_pairs={{0,1},{1,2},{2,3},{3,4},{4,5},{5,6},{6,7},{8,9},{9,10},{10,11},{11... | collective-permute-start | bytes 368648 | tf_op jit(solution)/shard_map/while/body/eval_jaxpr/ppermute | solution.py:18
  156.0 1.9 conditional.4
  163.1 5.2 collective-permute-start.1
  183.3 31.7 %collective-permute-start.1 = (bf16[16,3840]{1,0:T(8,128)(2,1)}, bf16[16,3840]{1,0:T(8,128)(2,1)}, u32[]{:S(2)}, u32[]{:S(2)}) collective-permute-start(bf16[16,3840]{1,0:T(8,128)(2,1)} %get-tuple-element.661), channel_id=1, source_target_pairs={{0,1},{1,2},{2,3},{3,4},{4,5},{5,6},{6,7},{8,9},{9,10},{10,11},{11... | collective-permute-start | bytes 368648 | tf_op jit(solution)/shard_map/while/body/eval_jaxpr/ppermute | solution.py:18
  222.9 8.1 %conditional.4 = (bf16[16,3840]{1,0:T(8,128)(2,1)}, bf16[16,3840]{1,0:T(8,128)(2,1)}, bf16[16,256]{1,0:T(8,128)(2,1)S(1)}, bf16[16,256]{1,0:T(8,128)(2,1)}) conditional(s32[]{:T(128)} %convert_element_type.144, () %tuple.95, (bf16[16,3840]{1,0:T(8,128)(2,1)S(1)}, bf16[2,4,16,3840]{3,2,1,0:T(8,128)(2,1)S(1)}, s32[]{:T(128)}, ...), branch_computations={%region_1.1_spmd, %region_2.6_spmd} | conditional | flops 95461472 | bytes 16450928 | solution.py:118
  222.9 2.4 slice_bitcast_fusion
  237.8 5.2 collective-permute-start.1
  250.9 8.1 %conditional.4 = (bf16[16,3840]{1,0:T(8,128)(2,1)}, bf16[16,3840]{1,0:T(8,128)(2,1)}, bf16[16,256]{1,0:T(8,128)(2,1)S(1)}, bf16[16,256]{1,0:T(8,128)(2,1)}) conditional(s32[]{:T(128)} %convert_element_type.144, () %tuple.95, (bf16[16,3840]{1,0:T(8,128)(2,1)S(1)}, bf16[2,4,16,3840]{3,2,1,0:T(8,128)(2,1)S(1)}, s32[]{:T(128)}, ...), branch_computations={%region_1.1_spmd, %region_2.6_spmd} | conditional | flops 95461472 | bytes 16450928 | solution.py:118
  250.9 2.4 slice_bitcast_fusion
  265.7 12.9 %collective-permute-start.1 = (bf16[16,3840]{1,0:T(8,128)(2,1)}, bf16[16,3840]{1,0:T(8,128)(2,1)}, u32[]{:S(2)}, u32[]{:S(2)}) collective-permute-start(bf16[16,3840]{1,0:T(8,128)(2,1)} %get-tuple-element.661), channel_id=1, source_target_pairs={{0,1},{1,2},{2,3},{3,4},{4,5},{5,6},{6,7},{8,9},{9,10},{10,11},{11... | collective-permute-start | bytes 368648 | tf_op jit(solution)/shard_map/while/body/eval_jaxpr/ppermute | solution.py:18
  286.6 8.1 %conditional.4 = (bf16[16,3840]{1,0:T(8,128)(2,1)}, bf16[16,3840]{1,0:T(8,128)(2,1)}, bf16[16,256]{1,0:T(8,128)(2,1)S(1)}, bf16[16,256]{1,0:T(8,128)(2,1)}) conditional(s32[]{:T(128)} %convert_element_type.144, () %tuple.95, (bf16[16,3840]{1,0:T(8,128)(2,1)S(1)}, bf16[2,4,16,3840]{3,2,1,0:T(8,128)(2,1)S(1)}, s32[]{:T(128)}, ...), branch_computations={%region_1.1_spmd, %region_2.6_spmd} | conditional | flops 95461472 | bytes 16450928 | solution.py:118
  286.6 2.4 slice_bitcast_fusion
  301.4 5.2 collective-permute-start.1
  314.5 8.1 %conditional.4 = (bf16[16,3840]{1,0:T(8,128)(2,1)}, bf16[16,3840]{1,0:T(8,128)(2,1)}, bf16[16,256]{1,0:T(8,128)(2,1)S(1)}, bf16[16,256]{1,0:T(8,128)(2,1)}) conditional(s32[]{:T(128)} %convert_element_type.144, () %tuple.95, (bf16[16,3840]{1,0:T(8,128)(2,1)S(1)}, bf16[2,4,16,3840]{3,2,1,0:T(8,128)(2,1)S(1)}, s32[]{:T(128)}, ...), branch_computations={%region_1.1_spmd, %region_2.6_spmd} | conditional | flops 95461472 | bytes 16450928 | solution.py:118
  314.6 2.4 slice_bitcast_fusion
  329.4 7.6 %copy.22 = bf16[2,4,16,3840]{2,1,0,3:T(4,128)(2,1)} copy(bf16[2,4,16,3840]{3,2,1,0:T(8,128)(2,1)S(1)} %pad_maximum_fusion.4) | data formatting | bytes 1966080 | tf_op jit(solution)/shard_map/stack | solution.py:72
  337.1 7.7 %copy.21 = bf16[2,4,16,3840]{2,1,0,3:T(4,128)(2,1)} copy(bf16[2,4,16,3840]{3,2,1,0:T(8,128)(2,1)S(1)} %pad_maximum_fusion.3) | data formatting | bytes 1966080 | tf_op jit(solution)/shard_map/stack | solution.py:72
  344.8 14.9 %fusion.29 = bf16[3840,2,1,2,4,16]{5,4,3,2,1,0:T(4,128)(2,1)} fusion(bf16[1,2,4,1,16,3840]{4,2,1,3,0,5:T(4,128)(2,1)} %bitcast.188, bf16[1,2,4,1,16,3840]{4,2,1,3,0,5:T(4,128)(2,1)} %bitcast.189), kind=kLoop, calls=%fused_computation.113 | loop fusion | flops 983040 | bytes 3932160
  359.7 19.2 %reshape.122 = bf16[4,2,122880]{2,1,0:T(2,128)(2,1)} reshape(bf16[3840,2,1,2,4,16]{5,4,3,2,1,0:T(4,128)(2,1)} %fusion.29) | data formatting | bytes 3932160
  379.0 5.1 all-to-all-start
  384.1 25.1 %all_gather.3 = bf16[2,2,4,4,16,256]{5,4,2,3,1,0:T(8,128)(2,1)S(1)} all-gather(bf16[2,2,4,1,16,256]{5,4,2,3,1,0:T(8,128)(2,1)S(1)} %pad_maximum_fusion.5), channel_id=1, replica_groups=mesh['dp'=4,'pipe'=8] {'dp'}, dimensions={3}, use_global_device_ids=true | all-gather | bytes 655360 | tf_op jit(solution)/shard_map/all_gather | solution.py:151
  409.2 13.2 %reshape.123 = bf16[3840,2,1,2,4,16]{5,4,3,2,1,0:T(4,128)(2,1)} reshape(bf16[4,2,122880]{2,1,0:T(2,128)(2,1)S(1)} %all-to-all-done) | data formatting | bytes 3932160
  422.4 21.0 %copy.24 = bf16[2,2,4,1,16,4,960]{6,4,2,5,3,1,0:T(8,128)(2,1)S(1)} copy(bf16[2,2,4,1,16,4,960]{4,2,1,0,6,5,3:T(4,128)(2,1)} %bitcast.187) | data formatting | bytes 3932160 | tf_op jit(solution)/shard_map/all_to_all | solution.py:150
  444.9 2.2 pad_maximum_fusion.2
  447.1 3.3 reduce_sum.102
  450.5 2.6 collective-permute-done.2
  453.1 23.8 %collective-permute-done.3 = bf16[960,512]{1,0:T(8,128)(2,1)S(1)} collective-permute-done((bf16[960,512]{1,0:T(8,128)(2,1)S(1)}, bf16[960,512]{1,0:T(8,128)(2,1)S(1)}, u32[]{:S(2)}, u32[]{:S(2)}) %collective-permute-start.3) | collective-permute-done | bytes 983072 | tf_op jit(solution)/shard_map/ppermute | solution.py:24
  481.2 40.6 %collective-permute-done.4 = bf16[960,512]{1,0:T(8,128)(2,1)S(1)} collective-permute-done((bf16[960,512]{1,0:T(8,128)(2,1)S(1)}, bf16[960,512]{1,0:T(8,128)(2,1)S(1)}, u32[]{:S(2)}, u32[]{:S(2)}) %collective-permute-start.4) | collective-permute-done | bytes 983072 | tf_op jit(solution)/shard_map/ppermute | solution.py:24
  521.8 4.2 convert_bitcast_fusion
  (427 shorter events, 235.8 us)
Async XLA Ops:
  0.6 5.9 %copy-start = (bf16[2,4,16,3840]{3,2,1,0:T(8,128)(2,1)S(1)}, bf16[2,4,16,3840]{3,2,1,0:T(8,128)(2,1)}, u32[]{:S(2)}) copy-start(bf16[2,4,16,3840]{3,2,1,0:T(8,128)(2,1)} %param.17) | copy-start | bytes 2949124
  0.6 5.8 %copy-start.1 = (bf16[1,2,4,16,3840]{4,3,2,1,0:T(8,128)(2,1)S(1)}, bf16[1,2,4,16,3840]{4,3,2,1,0:T(8,128)(2,1)}, u32[]{:S(2)}) copy-start(bf16[1,2,4,16,3840]{4,3,2,1,0:T(8,128)(2,1)} %param.16) | copy-start | bytes 2949124
  6.5 9.9 %collective-permute-start = (bf16[16,3840]{1,0:T(8,128)(2,1)}, bf16[16,3840]{1,0:T(8,128)(2,1)S(1)}, u32[]{:S(2)}, u32[]{:S(2)}) collective-permute-start(bf16[16,3840]{1,0:T(8,128)(2,1)} %get-tuple-element.660), channel_id=1, source_target_pairs={{1,0},{2,1},{3,2},{4,3},{5,4},{6,5},{7,6},{9,8},{10,9},{11,10},{12... | collective-permute-start | bytes 368648 | tf_op jit(solution)/shard_map/while/body/eval_jaxpr/ppermute | solution.py:18
  7.8 10.9 %collective-permute-start.1 = (bf16[16,3840]{1,0:T(8,128)(2,1)}, bf16[16,3840]{1,0:T(8,128)(2,1)}, u32[]{:S(2)}, u32[]{:S(2)}) collective-permute-start(bf16[16,3840]{1,0:T(8,128)(2,1)} %get-tuple-element.661), channel_id=1, source_target_pairs={{0,1},{1,2},{2,3},{3,4},{4,5},{5,6},{6,7},{8,9},{9,10},{10,11},{11... | collective-permute-start | bytes 368648 | tf_op jit(solution)/shard_map/while/body/eval_jaxpr/ppermute | solution.py:18
  16.4 0.7 copy-start.5
  19.4 1.9 copy-start.2
  32.9 9.9 %collective-permute-start = (bf16[16,3840]{1,0:T(8,128)(2,1)}, bf16[16,3840]{1,0:T(8,128)(2,1)S(1)}, u32[]{:S(2)}, u32[]{:S(2)}) collective-permute-start(bf16[16,3840]{1,0:T(8,128)(2,1)} %get-tuple-element.660), channel_id=1, source_target_pairs={{1,0},{2,1},{3,2},{4,3},{5,4},{6,5},{7,6},{9,8},{10,9},{11,10},{12... | collective-permute-start | bytes 368648 | tf_op jit(solution)/shard_map/while/body/eval_jaxpr/ppermute | solution.py:18
  34.2 10.9 %collective-permute-start.1 = (bf16[16,3840]{1,0:T(8,128)(2,1)}, bf16[16,3840]{1,0:T(8,128)(2,1)}, u32[]{:S(2)}, u32[]{:S(2)}) collective-permute-start(bf16[16,3840]{1,0:T(8,128)(2,1)} %get-tuple-element.661), channel_id=1, source_target_pairs={{0,1},{1,2},{2,3},{3,4},{4,5},{5,6},{6,7},{8,9},{9,10},{10,11},{11... | collective-permute-start | bytes 368648 | tf_op jit(solution)/shard_map/while/body/eval_jaxpr/ppermute | solution.py:18
  45.8 1.9 copy-start.2
  59.4 9.9 %collective-permute-start = (bf16[16,3840]{1,0:T(8,128)(2,1)}, bf16[16,3840]{1,0:T(8,128)(2,1)S(1)}, u32[]{:S(2)}, u32[]{:S(2)}) collective-permute-start(bf16[16,3840]{1,0:T(8,128)(2,1)} %get-tuple-element.660), channel_id=1, source_target_pairs={{1,0},{2,1},{3,2},{4,3},{5,4},{6,5},{7,6},{9,8},{10,9},{11,10},{12... | collective-permute-start | bytes 368648 | tf_op jit(solution)/shard_map/while/body/eval_jaxpr/ppermute | solution.py:18
  60.7 10.9 %collective-permute-start.1 = (bf16[16,3840]{1,0:T(8,128)(2,1)}, bf16[16,3840]{1,0:T(8,128)(2,1)}, u32[]{:S(2)}, u32[]{:S(2)}) collective-permute-start(bf16[16,3840]{1,0:T(8,128)(2,1)} %get-tuple-element.661), channel_id=1, source_target_pairs={{0,1},{1,2},{2,3},{3,4},{4,5},{5,6},{6,7},{8,9},{9,10},{10,11},{11... | collective-permute-start | bytes 368648 | tf_op jit(solution)/shard_map/while/body/eval_jaxpr/ppermute | solution.py:18
  72.3 1.9 copy-start.2
  85.9 11.2 %collective-permute-start = (bf16[16,3840]{1,0:T(8,128)(2,1)}, bf16[16,3840]{1,0:T(8,128)(2,1)S(1)}, u32[]{:S(2)}, u32[]{:S(2)}) collective-permute-start(bf16[16,3840]{1,0:T(8,128)(2,1)} %get-tuple-element.660), channel_id=1, source_target_pairs={{1,0},{2,1},{3,2},{4,3},{5,4},{6,5},{7,6},{9,8},{10,9},{11,10},{12... | collective-permute-start | bytes 368648 | tf_op jit(solution)/shard_map/while/body/eval_jaxpr/ppermute | solution.py:18
  87.2 12.2 %collective-permute-start.1 = (bf16[16,3840]{1,0:T(8,128)(2,1)}, bf16[16,3840]{1,0:T(8,128)(2,1)}, u32[]{:S(2)}, u32[]{:S(2)}) collective-permute-start(bf16[16,3840]{1,0:T(8,128)(2,1)} %get-tuple-element.661), channel_id=1, source_target_pairs={{0,1},{1,2},{2,3},{3,4},{4,5},{5,6},{6,7},{8,9},{9,10},{10,11},{11... | collective-permute-start | bytes 368648 | tf_op jit(solution)/shard_map/while/body/eval_jaxpr/ppermute | solution.py:18
  100.0 1.9 copy-start.2
  113.6 11.4 %collective-permute-start = (bf16[16,3840]{1,0:T(8,128)(2,1)}, bf16[16,3840]{1,0:T(8,128)(2,1)S(1)}, u32[]{:S(2)}, u32[]{:S(2)}) collective-permute-start(bf16[16,3840]{1,0:T(8,128)(2,1)} %get-tuple-element.660), channel_id=1, source_target_pairs={{1,0},{2,1},{3,2},{4,3},{5,4},{6,5},{7,6},{9,8},{10,9},{11,10},{12... | collective-permute-start | bytes 368648 | tf_op jit(solution)/shard_map/while/body/eval_jaxpr/ppermute | solution.py:18
  114.9 12.4 %collective-permute-start.1 = (bf16[16,3840]{1,0:T(8,128)(2,1)}, bf16[16,3840]{1,0:T(8,128)(2,1)}, u32[]{:S(2)}, u32[]{:S(2)}) collective-permute-start(bf16[16,3840]{1,0:T(8,128)(2,1)} %get-tuple-element.661), channel_id=1, source_target_pairs={{0,1},{1,2},{2,3},{3,4},{4,5},{5,6},{6,7},{8,9},{9,10},{10,11},{11... | collective-permute-start | bytes 368648 | tf_op jit(solution)/shard_map/while/body/eval_jaxpr/ppermute | solution.py:18
  128.0 1.9 copy-start.2
  133.8 19.2 %collective-permute-start = (bf16[16,3840]{1,0:T(8,128)(2,1)}, bf16[16,3840]{1,0:T(8,128)(2,1)S(1)}, u32[]{:S(2)}, u32[]{:S(2)}) collective-permute-start(bf16[16,3840]{1,0:T(8,128)(2,1)} %get-tuple-element.660), channel_id=1, source_target_pairs={{1,0},{2,1},{3,2},{4,3},{5,4},{6,5},{7,6},{9,8},{10,9},{11,10},{12... | collective-permute-start | bytes 368648 | tf_op jit(solution)/shard_map/while/body/eval_jaxpr/ppermute | solution.py:18
  135.1 20.1 %collective-permute-start.1 = (bf16[16,3840]{1,0:T(8,128)(2,1)}, bf16[16,3840]{1,0:T(8,128)(2,1)}, u32[]{:S(2)}, u32[]{:S(2)}) collective-permute-start(bf16[16,3840]{1,0:T(8,128)(2,1)} %get-tuple-element.661), channel_id=1, source_target_pairs={{0,1},{1,2},{2,3},{3,4},{4,5},{5,6},{6,7},{8,9},{9,10},{10,11},{11... | collective-permute-start | bytes 368648 | tf_op jit(solution)/shard_map/while/body/eval_jaxpr/ppermute | solution.py:18
  156.0 1.9 copy-start.2
  161.8 11.4 %collective-permute-start = (bf16[16,3840]{1,0:T(8,128)(2,1)}, bf16[16,3840]{1,0:T(8,128)(2,1)S(1)}, u32[]{:S(2)}, u32[]{:S(2)}) collective-permute-start(bf16[16,3840]{1,0:T(8,128)(2,1)} %get-tuple-element.660), channel_id=1, source_target_pairs={{1,0},{2,1},{3,2},{4,3},{5,4},{6,5},{7,6},{9,8},{10,9},{11,10},{12... | collective-permute-start | bytes 368648 | tf_op jit(solution)/shard_map/while/body/eval_jaxpr/ppermute | solution.py:18
  163.1 12.4 %collective-permute-start.1 = (bf16[16,3840]{1,0:T(8,128)(2,1)}, bf16[16,3840]{1,0:T(8,128)(2,1)}, u32[]{:S(2)}, u32[]{:S(2)}) collective-permute-start(bf16[16,3840]{1,0:T(8,128)(2,1)} %get-tuple-element.661), channel_id=1, source_target_pairs={{0,1},{1,2},{2,3},{3,4},{4,5},{5,6},{6,7},{8,9},{9,10},{10,11},{11... | collective-permute-start | bytes 368648 | tf_op jit(solution)/shard_map/while/body/eval_jaxpr/ppermute | solution.py:18
  176.2 1.9 copy-start.2
  182.0 37.9 %collective-permute-start = (bf16[16,3840]{1,0:T(8,128)(2,1)}, bf16[16,3840]{1,0:T(8,128)(2,1)S(1)}, u32[]{:S(2)}, u32[]{:S(2)}) collective-permute-start(bf16[16,3840]{1,0:T(8,128)(2,1)} %get-tuple-element.660), channel_id=1, source_target_pairs={{1,0},{2,1},{3,2},{4,3},{5,4},{6,5},{7,6},{9,8},{10,9},{11,10},{12... | collective-permute-start | bytes 368648 | tf_op jit(solution)/shard_map/while/body/eval_jaxpr/ppermute | solution.py:18
  183.3 38.9 %collective-permute-start.1 = (bf16[16,3840]{1,0:T(8,128)(2,1)}, bf16[16,3840]{1,0:T(8,128)(2,1)}, u32[]{:S(2)}, u32[]{:S(2)}) collective-permute-start(bf16[16,3840]{1,0:T(8,128)(2,1)} %get-tuple-element.661), channel_id=1, source_target_pairs={{0,1},{1,2},{2,3},{3,4},{4,5},{5,6},{6,7},{8,9},{9,10},{10,11},{11... | collective-permute-start | bytes 368648 | tf_op jit(solution)/shard_map/while/body/eval_jaxpr/ppermute | solution.py:18
  222.9 8.1 %copy-start.2 = (bf16[1,16,3840]{2,1,0:T(8,128)(2,1)S(1)}, bf16[1,16,3840]{2,1,0:T(8,128)(2,1)}, u32[]{:S(2)}) copy-start(bf16[1,16,3840]{2,1,0:T(8,128)(2,1)} %get-tuple-element.609) | copy-start | bytes 368644 | tf_op jit(solution)/shard_map/while
  236.5 11.4 %collective-permute-start = (bf16[16,3840]{1,0:T(8,128)(2,1)}, bf16[16,3840]{1,0:T(8,128)(2,1)S(1)}, u32[]{:S(2)}, u32[]{:S(2)}) collective-permute-start(bf16[16,3840]{1,0:T(8,128)(2,1)} %get-tuple-element.660), channel_id=1, source_target_pairs={{1,0},{2,1},{3,2},{4,3},{5,4},{6,5},{7,6},{9,8},{10,9},{11,10},{12... | collective-permute-start | bytes 368648 | tf_op jit(solution)/shard_map/while/body/eval_jaxpr/ppermute | solution.py:18
  237.8 12.4 %collective-permute-start.1 = (bf16[16,3840]{1,0:T(8,128)(2,1)}, bf16[16,3840]{1,0:T(8,128)(2,1)}, u32[]{:S(2)}, u32[]{:S(2)}) collective-permute-start(bf16[16,3840]{1,0:T(8,128)(2,1)} %get-tuple-element.661), channel_id=1, source_target_pairs={{0,1},{1,2},{2,3},{3,4},{4,5},{5,6},{6,7},{8,9},{9,10},{10,11},{11... | collective-permute-start | bytes 368648 | tf_op jit(solution)/shard_map/while/body/eval_jaxpr/ppermute | solution.py:18
  250.9 8.1 %copy-start.2 = (bf16[1,16,3840]{2,1,0:T(8,128)(2,1)S(1)}, bf16[1,16,3840]{2,1,0:T(8,128)(2,1)}, u32[]{:S(2)}) copy-start(bf16[1,16,3840]{2,1,0:T(8,128)(2,1)} %get-tuple-element.609) | copy-start | bytes 368644 | tf_op jit(solution)/shard_map/while
  264.4 19.2 %collective-permute-start = (bf16[16,3840]{1,0:T(8,128)(2,1)}, bf16[16,3840]{1,0:T(8,128)(2,1)S(1)}, u32[]{:S(2)}, u32[]{:S(2)}) collective-permute-start(bf16[16,3840]{1,0:T(8,128)(2,1)} %get-tuple-element.660), channel_id=1, source_target_pairs={{1,0},{2,1},{3,2},{4,3},{5,4},{6,5},{7,6},{9,8},{10,9},{11,10},{12... | collective-permute-start | bytes 368648 | tf_op jit(solution)/shard_map/while/body/eval_jaxpr/ppermute | solution.py:18
  265.7 20.1 %collective-permute-start.1 = (bf16[16,3840]{1,0:T(8,128)(2,1)}, bf16[16,3840]{1,0:T(8,128)(2,1)}, u32[]{:S(2)}, u32[]{:S(2)}) collective-permute-start(bf16[16,3840]{1,0:T(8,128)(2,1)} %get-tuple-element.661), channel_id=1, source_target_pairs={{0,1},{1,2},{2,3},{3,4},{4,5},{5,6},{6,7},{8,9},{9,10},{10,11},{11... | collective-permute-start | bytes 368648 | tf_op jit(solution)/shard_map/while/body/eval_jaxpr/ppermute | solution.py:18
  286.6 8.1 %copy-start.2 = (bf16[1,16,3840]{2,1,0:T(8,128)(2,1)S(1)}, bf16[1,16,3840]{2,1,0:T(8,128)(2,1)}, u32[]{:S(2)}) copy-start(bf16[1,16,3840]{2,1,0:T(8,128)(2,1)} %get-tuple-element.609) | copy-start | bytes 368644 | tf_op jit(solution)/shard_map/while
  300.1 11.4 %collective-permute-start = (bf16[16,3840]{1,0:T(8,128)(2,1)}, bf16[16,3840]{1,0:T(8,128)(2,1)S(1)}, u32[]{:S(2)}, u32[]{:S(2)}) collective-permute-start(bf16[16,3840]{1,0:T(8,128)(2,1)} %get-tuple-element.660), channel_id=1, source_target_pairs={{1,0},{2,1},{3,2},{4,3},{5,4},{6,5},{7,6},{9,8},{10,9},{11,10},{12... | collective-permute-start | bytes 368648 | tf_op jit(solution)/shard_map/while/body/eval_jaxpr/ppermute | solution.py:18
  301.4 12.4 %collective-permute-start.1 = (bf16[16,3840]{1,0:T(8,128)(2,1)}, bf16[16,3840]{1,0:T(8,128)(2,1)}, u32[]{:S(2)}, u32[]{:S(2)}) collective-permute-start(bf16[16,3840]{1,0:T(8,128)(2,1)} %get-tuple-element.661), channel_id=1, source_target_pairs={{0,1},{1,2},{2,3},{3,4},{4,5},{5,6},{6,7},{8,9},{9,10},{10,11},{11... | collective-permute-start | bytes 368648 | tf_op jit(solution)/shard_map/while/body/eval_jaxpr/ppermute | solution.py:18
  314.5 8.1 %copy-start.2 = (bf16[1,16,3840]{2,1,0:T(8,128)(2,1)S(1)}, bf16[1,16,3840]{2,1,0:T(8,128)(2,1)}, u32[]{:S(2)}) copy-start(bf16[1,16,3840]{2,1,0:T(8,128)(2,1)} %get-tuple-element.609) | copy-start | bytes 368644 | tf_op jit(solution)/shard_map/while
  329.4 7.6 %copy-start.3 = (bf16[4,16,3840]{2,1,0:T(8,128)(2,1)S(1)}, bf16[4,16,3840]{2,1,0:T(8,128)(2,1)}, u32[]{:S(2)}) copy-start(bf16[4,16,3840]{2,1,0:T(8,128)(2,1)} %get-tuple-element.388) | copy-start | bytes 1474564
  329.4 7.6 %copy-start.4 = (bf16[4,16,3840]{2,1,0:T(8,128)(2,1)S(1)}, bf16[4,16,3840]{2,1,0:T(8,128)(2,1)}, u32[]{:S(2)}) copy-start(bf16[4,16,3840]{2,1,0:T(8,128)(2,1)} %get-tuple-element.387) | copy-start | bytes 1474564
  379.0 5.1 copy-start.10
  379.0 5.1 copy-start.11
  379.0 30.3 %all-to-all-start = ((bf16[4,2,122880]{2,1,0:T(2,128)(2,1)}), bf16[4,2,122880]{2,1,0:T(2,128)(2,1)S(1)}, u32[]{:S(2)}, u32[]{:S(2)}) async-start(bf16[4,2,122880]{2,1,0:T(2,128)(2,1)} %reshape.122), calls=%async_computation | async-start | bytes 3932160 | tf_op jit(solution)/shard_map/all_to_all | solution.py:150
  409.2 34.9 %copy-start.9 = (bf16[2,2,4,4,16,256]{5,4,2,3,1,0:T(8,128)(2,1)}, bf16[2,2,4,4,16,256]{5,4,2,3,1,0:T(8,128)(2,1)S(1)}, u32[]{:S(2)}) copy-start(bf16[2,2,4,4,16,256]{5,4,2,3,1,0:T(8,128)(2,1)S(1)} %all_gather.3) | copy-start | bytes 1572868
  450.4 2.6 collective-permute-start.2
  453.1 23.8 %collective-permute-start.3 = (bf16[960,512]{1,0:T(8,128)(2,1)S(1)}, bf16[960,512]{1,0:T(8,128)(2,1)S(1)}, u32[]{:S(2)}, u32[]{:S(2)}) collective-permute-start(bf16[960,512]{1,0:T(8,128)(2,1)S(1)} %collective-permute-done.2), channel_id=1, source_target_pairs={{0,2},{1,3},{2,0},{3,1},{4,6},{5,7},{6,4},{7,5},{8,10},{9,11},{10,... | collective-permute-start | bytes 2949128 | tf_op jit(solution)/shard_map/ppermute | solution.py:24
  476.9 44.9 %collective-permute-start.4 = (bf16[960,512]{1,0:T(8,128)(2,1)S(1)}, bf16[960,512]{1,0:T(8,128)(2,1)S(1)}, u32[]{:S(2)}, u32[]{:S(2)}) collective-permute-start(bf16[960,512]{1,0:T(8,128)(2,1)S(1)} %collective-permute-done.3), channel_id=1, source_target_pairs={{0,4},{1,5},{2,6},{3,7},{4,0},{5,1},{6,2},{7,3},{8,12},{9,13},{10,... | collective-permute-start | bytes 2949128 | tf_op jit(solution)/shard_map/ppermute | solution.py:24
  480.5 41.3 %copy-start.6 = (f32[1,960,512]{2,1,0:T(8,128)S(1)}, f32[1,960,512]{2,1,0:T(8,128)}, u32[]{:S(2)}) copy-start(f32[1,960,512]{2,1,0:T(8,128)} %param.13) | copy-start | bytes 5898244
  480.5 41.3 %copy-start.7 = (bf16[1,960,512]{2,1,0:T(8,128)(2,1)S(1)}, bf16[1,960,512]{2,1,0:T(8,128)(2,1)}, u32[]{:S(2)}) copy-start(bf16[1,960,512]{2,1,0:T(8,128)(2,1)} %param.15) | copy-start | bytes 2949124
  480.5 41.3 %copy-start.8 = (bf16[1,960,512]{2,1,0:T(8,128)(2,1)S(1)}, bf16[1,960,512]{2,1,0:T(8,128)(2,1)}, u32[]{:S(2)}) copy-start(bf16[1,960,512]{2,1,0:T(8,128)(2,1)} %param.14) | copy-start | bytes 2949124
  (10 other events, 6.5 us)
where the time goes:
time: 531 us; the launch traced here: 526 us
  local copies, waits for them, and re-layouts  182 us (34%)
  starting transfers between devices  113 us (21%)
  other arithmetic  106 us (20%)
  waiting for transfers between devices  67 us (13%)
  matrix products  30.2 us (6%)
  blocking collectives  25.1 us (5%)
    ppermute x22, starting transfers between devices, from_behind(): return lax.ppermute(array, axis, pairs)  108 us
    ppermute x3, waiting for transfers between devices, from_partner(): return lax.ppermute(value, axis, pairs)  67 us
    dynamic_update_slice x66, other arithmetic, store_slot(): return lax.dynamic_update_index_in_dim(stored, chosen, clipped, 0)  60 us
    dynamic_slice x77, local copies, waits for them, and re-layouts, store_slot(): previous = lax.dynamic_index_in_dim(stored, clipped, 0, keepdims=False)  53.5 us
    unnamed x22, local copies, waits for them, and re-layouts  32.5 us
    another operation x58, local copies, waits for them, and re-layouts  28.1 us
    all_gather x1, blocking collectives, shards(): narrow_recv = lax.all_gather(narrow_both, 'dp', axis=3, tiled=True)  25.1 us
    all_to_all x1, local copies, waits for them, and re-layouts, shards(): lax.all_to_all(wide_both, 'dp', split_axis=5, concat_axis=3, tiled=True)  21 us
  transfers between devices with their start and end apart: 26, of which 3 were waited for; matrix products, arithmetic and copies ran while one was open for 14% of the time, Pallas kernels for 0%

commit v1 on v0

v1 whole, which is shorter than its diff:
```python
import jax
import jax.numpy as jnp
from jax import lax
from jax.sharding import PartitionSpec as P

norm_epsilon = 1e-06
first_decay = 0.9
second_decay = 0.95
adam_epsilon = 1e-08
learn_rate = 0.00022
weight_decay = 0.1
step_count = 100.0


def adamw(master, moment1, moment2, gradient):
    first_new = first_decay * moment1.astype(jnp.float32) + (1.0 - first_decay) * gradient
    second_new = (
        second_decay * moment2.astype(jnp.float32) + (1.0 - second_decay) * gradient * gradient
    )
    first_hat = first_new / (1.0 - first_decay**step_count)
    second_hat = second_new / (1.0 - second_decay**step_count)
    updated = master - learn_rate * (
        first_hat / (jnp.sqrt(second_hat) + adam_epsilon) + weight_decay * master
    )
    return (updated, first_new.astype(jnp.bfloat16), second_new.astype(jnp.bfloat16))


def prepare(x, down_proj):
    values = x.astype(jnp.float32)
    row_scale = lax.rsqrt(jnp.mean(values * values, axis=-1, keepdims=True) + norm_epsilon)
    normed = (values * row_scale).astype(jnp.bfloat16)
    latent = jnp.einsum("mtd,dk->mtk", normed, down_proj, preferred_element_type=jnp.float32)
    return row_scale, normed, latent


def replica_pieces(array):
    count = lax.axis_size("dp")
    me = lax.axis_index("dp")
    width = array.shape[-1] // count

    def piece(owner):
        return lax.dynamic_slice_in_dim(array, owner * width, width, array.ndim - 1)

    pieces = [piece(me)]
    for apart in range(1, count):
        pairs = [(i, (i + apart) % count) for i in range(count)]
        pieces.append(lax.ppermute(piece(lax.rem(me + apart, count)), "dp", pairs))
    return pieces


def replica_rows(array):
    count = lax.axis_size("dp")
    rows = [array]
    for apart in range(1, count):
        pairs = [(i, (i + apart) % count) for i in range(count)]
        rows.append(lax.ppermute(array, "dp", pairs))
    return rows


def shards(weights, master, moment1, moment2, saved, cotangent):
    sections = lax.axis_size("pipe")
    position = lax.axis_index("pipe")
    micro, rows, features = saved.shape[2:]
    section_weights = weights[0, 0]
    rank = section_weights.shape[1] // 2
    down_proj = section_weights[:, :rank]
    up_proj = section_weights[:, rank:]

    swap = [(i, sections - 1 - i) for i in range(sections)]
    x_ahead = saved[0, 0]
    x_behind = lax.ppermute(saved[0, 1], "pipe", swap)
    scale_a, normed_a, latent_a = prepare(x_ahead, down_proj)
    scale_b, normed_b, latent_b = prepare(x_behind, down_proj)
    x = jnp.concatenate([x_ahead, x_behind], axis=1)
    row_scale = jnp.concatenate([scale_a, scale_b], axis=1)
    latent = jnp.concatenate([latent_a, latent_b], axis=1)
    latent_scale = lax.rsqrt(jnp.mean(latent * latent, axis=-1, keepdims=True) + norm_epsilon)
    latent_act = (latent * latent_scale).astype(jnp.bfloat16)
    entries = jnp.concatenate([cotangent[0], cotangent[1]], axis=1)

    down_pairs = [(i, i - 1) for i in range(1, sections)]
    first_tick = sections - 1 - position
    received, latents = [], []
    sent = None
    for tick in range(sections - 1 + micro):
        index = jnp.clip(tick - first_tick, 0, micro - 1)

        def at(array):
            return lax.dynamic_index_in_dim(array, index, 0, keepdims=False)

        if sent is None:
            grad_out = entries[0]
        else:
            grad_out = lax.ppermute(sent, "pipe", down_pairs)
            if tick < micro:
                grad_out = jnp.where(position == sections - 1, entries[tick], grad_out)
        x_now, scale_now, latent_now, lscale_now = at(x), at(row_scale), at(latent), at(latent_scale)
        grad_act = jnp.dot(grad_out, up_proj, preferred_element_type=jnp.float32)
        grad_latent = lscale_now * grad_act - latent_now * lscale_now**3 * jnp.mean(
            latent_now * grad_act, axis=-1, keepdims=True
        )
        grad_latent = grad_latent.astype(jnp.bfloat16)
        along = jnp.sum(latent_now * grad_latent.astype(jnp.float32), axis=-1, keepdims=True)
        along = along * (scale_now * scale_now / features)
        grad_normed = jnp.dot(grad_latent, down_proj.T, preferred_element_type=jnp.float32)
        sent = (
            grad_out.astype(jnp.float32)
            + scale_now * grad_normed
            - x_now.astype(jnp.float32) * along
        ).astype(jnp.bfloat16)
        received.append(grad_out)
        latents.append(grad_latent)

    grad_out = lax.dynamic_slice_in_dim(jnp.stack(received), first_tick, micro, 0)
    grad_latent = lax.dynamic_slice_in_dim(jnp.stack(latents), first_tick, micro, 0)

    def flat(array):
        return array.reshape(-1, array.shape[-1])

    normed = jnp.concatenate([normed_a, normed_b], axis=1)
    normed_all = jnp.concatenate(replica_pieces(flat(normed)))
    narrow = jnp.concatenate([flat(grad_latent), flat(latent_act)], axis=1)
    narrow_all = jnp.concatenate(replica_rows(narrow))
    wide_all = jnp.concatenate(replica_pieces(flat(grad_out)))
    down_part = jnp.einsum("td,tk->dk", normed_all, narrow_all[:, :rank], preferred_element_type=jnp.float32)
    up_part = jnp.einsum("td,tk->dk", wide_all, narrow_all[:, rank:], preferred_element_type=jnp.float32)
    gradient = jnp.concatenate([down_part, up_part], axis=1)
    new_master, new_first, new_second = adamw(master[0], moment1[0], moment2[0], gradient)
    return (new_master[None], new_first[None], new_second[None])


def solution(mesh):
    return jax.shard_map(
        shards,
        mesh=mesh,
        in_specs=(
            P("pipe", None, None, None),
            P("pipe", "dp", None),
            P("pipe", "dp", None),
            P("pipe", "dp", None),
            P("pipe", None, None, "dp", None),
            P(None, None, "dp", None),
        ),
        out_specs=(P("pipe", "dp", None), P("pipe", "dp", None), P("pipe", "dp", None)),
        check_vma=False,
    )
```

time: 531 us -> 161 us (0.30)
  the two profiles are of different devices: /device:TPU:0 before, /device:TPU:16 now
where the time goes in v1:
time: 161 us
  waiting for transfers between devices  60 us (37%)
  starting transfers between devices  50.9 us (32%)
  matrix products  19.8 us (12%)
  local copies, waits for them, and re-layouts  14.4 us (9%)
  other arithmetic  14.3 us (9%)
    ppermute x10, starting transfers between devices, shards(): grad_out = lax.ppermute(sent, 'pipe', down_pairs)  35.7 us
    ppermute x10, waiting for transfers between devices, shards(): grad_out = lax.ppermute(sent, 'pipe', down_pairs)  28.4 us
    ppermute x1, waiting for transfers between devices, shards(): x_behind = lax.ppermute(saved[0, 1], 'pipe', swap)  19 us
    ppermute x6, waiting for transfers between devices, replica_pieces(): pieces.append(lax.ppermute(piece(lax.rem(me + apart, count)), 'dp', pairs))  10.7 us
    dot_general x10, matrix products, shards(): jnp.dot(grad_latent, down_proj.T, preferred_element_type=jnp.float32)  9.73 us
    ppermute x6, starting transfers between devices, replica_pieces(): pieces.append(lax.ppermute(piece(lax.rem(me + apart, count)), 'dp', pairs))  9.45 us
    dot_general x11, matrix products, shards(): grad_act = jnp.dot(grad_out, up_proj, preferred_element_type=jnp.float32)  8.23 us
    unnamed x14, other arithmetic  6.28 us
  transfers between devices with their start and end apart: 20, of which 14 were waited for; matrix products, arithmetic and copies ran while one was open for 17% of the time, Pallas kernels for 0%

profile of v1, /device:TPU:16, one launch (start us, length us, event | category | flops | bytes accessed | tf_op | source)
XLA Modules:
  0.0 160.7 jit_solution(14652847527336578320)
XLA Ops:
  0.6 1.3 slice_bitcast_fusion.4
  2.5 1.2 slice_bitcast_fusion.2
  3.7 2.4 %slice_bitcast_fusion = bf16[3840,512]{1,0:T(8,128)(2,1)S(1)} fusion(bf16[1,2,3840,512]{3,2,1,0:T(8,128)(2,1)} %param.6), kind=kLoop, calls=%fused_computation.13 | loop fusion | bytes 7864320 | tf_op jit(solution)/shard_map/squeeze | solution.py:64
  7.1 19.0 %collective-permute-done = bf16[4,16,3840]{2,1,0:T(8,128)(2,1)S(1)} collective-permute-done((bf16[4,16,3840]{2,1,0:T(8,128)(2,1)S(1)}, bf16[4,16,3840]{2,1,0:T(8,128)(2,1)S(1)}, u32[]{:S(2)}, u32[]{:S(2)}) %collective-permute-start) | collective-permute-done | bytes 491552 | tf_op jit(solution)/shard_map/ppermute | solution.py:71
  28.8 2.0 %collective-permute-start.4 = (bf16[32,3840]{1,0:T(8,128)(2,1)S(1)}, bf16[32,3840]{1,0:T(8,128)(2,1)S(1)}, u32[]{:S(2)}, u32[]{:S(2)}) collective-permute-start(bf16[32,3840]{1,0:T(8,128)(2,1)S(1)} %fusion.2), channel_id=1, source_target_pairs={{1,0},{2,1},{3,2},{4,3},{5,4},{6,5},{7,6},{9,8},{10,9},{11,10},{12... | collective-permute-start | bytes 737288 | tf_op jit(solution)/shard_map/ppermute | solution.py:94
  31.5 3.0 %collective-permute-done.4 = bf16[32,3840]{1,0:T(8,128)(2,1)S(1)} collective-permute-done((bf16[32,3840]{1,0:T(8,128)(2,1)S(1)}, bf16[32,3840]{1,0:T(8,128)(2,1)S(1)}, u32[]{:S(2)}, u32[]{:S(2)}) %collective-permute-start.4) | collective-permute-done | bytes 245792 | tf_op jit(solution)/shard_map/ppermute | solution.py:94
  34.5 0.7 bitcast_dynamic-update-slice_fusion.9
  36.6 1.4 fusion.45
  38.1 3.8 %collective-permute-start.5 = (bf16[32,3840]{1,0:T(8,128)(2,1)}, bf16[32,3840]{1,0:T(8,128)(2,1)S(1)}, u32[]{:S(2)}, u32[]{:S(2)}) collective-permute-start(bf16[32,3840]{1,0:T(8,128)(2,1)} %fusion.45), channel_id=1, source_target_pairs={{1,0},{2,1},{3,2},{4,3},{5,4},{6,5},{7,6},{9,8},{10,9},{11,10},{12... | collective-permute-start | bytes 737288 | tf_op jit(solution)/shard_map/ppermute | solution.py:94
  41.9 4.0 %collective-permute-done.5 = bf16[32,3840]{1,0:T(8,128)(2,1)S(1)} collective-permute-done((bf16[32,3840]{1,0:T(8,128)(2,1)}, bf16[32,3840]{1,0:T(8,128)(2,1)S(1)}, u32[]{:S(2)}, u32[]{:S(2)}) %collective-permute-start.5) | collective-permute-done | bytes 245792 | tf_op jit(solution)/shard_map/ppermute | solution.py:94
  45.9 0.8 bitcast_dynamic-update-slice_fusion.8
  46.7 2.4 %fusion.144 = f32[32,256]{1,0:T(8,128)S(1)} fusion(bf16[32,3840]{1,0:T(8,128)(2,1)S(1)} %get-tuple-element.76, bf16[3840,512]{1,0:T(8,128)(2,1)} %copy-done), kind=kOutput, calls=%fused_computation.355 | convolution fusion | flops 62914560 | bytes 2244608 | tf_op jit(solution)/shard_map/dot_general | solution.py:98
  50.1 0.7 fusion.43
  50.8 3.7 %collective-permute-start.6 = (bf16[32,3840]{1,0:T(8,128)(2,1)S(1)}, bf16[32,3840]{1,0:T(8,128)(2,1)S(1)}, u32[]{:S(2)}, u32[]{:S(2)}) collective-permute-start(bf16[32,3840]{1,0:T(8,128)(2,1)S(1)} %fusion.43), channel_id=1, source_target_pairs={{1,0},{2,1},{3,2},{4,3},{5,4},{6,5},{7,6},{9,8},{10,9},{11,10},{12... | collective-permute-start | bytes 737288 | tf_op jit(solution)/shard_map/ppermute | solution.py:94
  54.6 3.6 %collective-permute-done.6 = bf16[32,3840]{1,0:T(8,128)(2,1)S(1)} collective-permute-done((bf16[32,3840]{1,0:T(8,128)(2,1)S(1)}, bf16[32,3840]{1,0:T(8,128)(2,1)S(1)}, u32[]{:S(2)}, u32[]{:S(2)}) %collective-permute-start.6) | collective-permute-done | bytes 245792 | tf_op jit(solution)/shard_map/ppermute | solution.py:94
  58.2 0.8 bitcast_dynamic-update-slice_fusion.7
  60.4 0.7 fusion.41
  61.1 3.8 %collective-permute-start.7 = (bf16[32,3840]{1,0:T(8,128)(2,1)S(1)}, bf16[32,3840]{1,0:T(8,128)(2,1)S(1)}, u32[]{:S(2)}, u32[]{:S(2)}) collective-permute-start(bf16[32,3840]{1,0:T(8,128)(2,1)S(1)} %fusion.41), channel_id=1, source_target_pairs={{1,0},{2,1},{3,2},{4,3},{5,4},{6,5},{7,6},{9,8},{10,9},{11,10},{12... | collective-permute-start | bytes 737288 | tf_op jit(solution)/shard_map/ppermute | solution.py:94
  65.7 2.4 %collective-permute-start.3 = (bf16[128,960]{1,0:T(8,128)(2,1)S(1)}, bf16[128,960]{1,0:T(8,128)(2,1)S(1)}, u32[]{:S(2)}, u32[]{:S(2)}) collective-permute-start(bf16[128,960]{1,0:T(8,128)(2,1)S(1)} %get-tuple-element.95), channel_id=1, source_target_pairs={{0,24},{8,0},{16,8},{24,16},{1,25},{9,1},{17,9},{25,17},{2,26},{10... | collective-permute-start | bytes 737288 | tf_op jit(solution)/shard_map/ppermute | solution.py:47
  69.4 2.0 %fusion.140 = f32[32,256]{1,0:T(8,128)S(1)} fusion(bf16[32,3840]{1,0:T(8,128)(2,1)S(1)} %collective-permute-done.7, bf16[3840,512]{1,0:T(8,128)(2,1)} %copy-done), kind=kOutput, calls=%fused_computation.351 | convolution fusion | flops 62914560 | bytes 2244608 | tf_op jit(solution)/shard_map/dot_general | solution.py:98
  71.8 2.4 %fusion.39 = bf16[32,3840]{1,0:T(8,128)(2,1)S(1)} fusion(bf16[32,3840]{1,0:T(8,128)(2,1)S(1)} %collective-permute-done.7, s32[]{:T(128)S(6)} %min.38, bf16[4,16,3840]{2,1,0:T(8,128)(2,1)S(1)} %get-tuple-element.102, bf16[4,16,3840]{2,1,0:T(8,128)(2,1)S(1)} %collective-permute-done, f32[32]{0:T(128)S(1)} %get-tuple-element.55, ...), kind=kOutput, calls=%fused_computation.94 | convolution fusion | flops 64266240 | bytes 3457284 | tf_op jit(solution)/shard_map/dot_general | solution.py:105
  74.2 3.4 %collective-permute-start.8 = (bf16[32,3840]{1,0:T(8,128)(2,1)S(1)}, bf16[32,3840]{1,0:T(8,128)(2,1)S(1)}, u32[]{:S(2)}, u32[]{:S(2)}) collective-permute-start(bf16[32,3840]{1,0:T(8,128)(2,1)S(1)} %fusion.39), channel_id=1, source_target_pairs={{1,0},{2,1},{3,2},{4,3},{5,4},{6,5},{7,6},{9,8},{10,9},{11,10},{12... | collective-permute-start | bytes 737288 | tf_op jit(solution)/shard_map/ppermute | solution.py:94
  78.3 3.0 %collective-permute-done.8 = bf16[32,3840]{1,0:T(8,128)(2,1)S(1)} collective-permute-done((bf16[32,3840]{1,0:T(8,128)(2,1)S(1)}, bf16[32,3840]{1,0:T(8,128)(2,1)S(1)}, u32[]{:S(2)}, u32[]{:S(2)}) %collective-permute-start.8) | collective-permute-done | bytes 245792 | tf_op jit(solution)/shard_map/ppermute | solution.py:94
  82.1 0.7 fusion.37
  82.8 3.8 %collective-permute-start.9 = (bf16[32,3840]{1,0:T(8,128)(2,1)S(1)}, bf16[32,3840]{1,0:T(8,128)(2,1)S(1)}, u32[]{:S(2)}, u32[]{:S(2)}) collective-permute-start(bf16[32,3840]{1,0:T(8,128)(2,1)S(1)} %fusion.37), channel_id=1, source_target_pairs={{1,0},{2,1},{3,2},{4,3},{5,4},{6,5},{7,6},{9,8},{10,9},{11,10},{12... | collective-permute-start | bytes 737288 | tf_op jit(solution)/shard_map/ppermute | solution.py:94
  87.3 3.0 %collective-permute-done.9 = bf16[32,3840]{1,0:T(8,128)(2,1)S(1)} collective-permute-done((bf16[32,3840]{1,0:T(8,128)(2,1)S(1)}, bf16[32,3840]{1,0:T(8,128)(2,1)S(1)}, u32[]{:S(2)}, u32[]{:S(2)}) %collective-permute-start.9) | collective-permute-done | bytes 245792 | tf_op jit(solution)/shard_map/ppermute | solution.py:94
  91.1 0.7 fusion.35
  91.8 3.8 %collective-permute-start.10 = (bf16[32,3840]{1,0:T(8,128)(2,1)S(1)}, bf16[32,3840]{1,0:T(8,128)(2,1)S(1)}, u32[]{:S(2)}, u32[]{:S(2)}) collective-permute-start(bf16[32,3840]{1,0:T(8,128)(2,1)S(1)} %fusion.35), channel_id=1, source_target_pairs={{1,0},{2,1},{3,2},{4,3},{5,4},{6,5},{7,6},{9,8},{10,9},{11,10},{12... | collective-permute-start | bytes 737288 | tf_op jit(solution)/shard_map/ppermute | solution.py:94
  95.7 0.7 bitcast_dynamic-update-slice_fusion.4
  96.4 3.0 %collective-permute-done.10 = bf16[32,3840]{1,0:T(8,128)(2,1)S(1)} collective-permute-done((bf16[32,3840]{1,0:T(8,128)(2,1)S(1)}, bf16[32,3840]{1,0:T(8,128)(2,1)S(1)}, u32[]{:S(2)}, u32[]{:S(2)}) %collective-permute-start.10) | collective-permute-done | bytes 245792 | tf_op jit(solution)/shard_map/ppermute | solution.py:94
  100.9 3.8 %collective-permute-start.11 = (bf16[32,3840]{1,0:T(8,128)(2,1)S(1)}, bf16[32,3840]{1,0:T(8,128)(2,1)S(1)}, u32[]{:S(2)}, u32[]{:S(2)}) collective-permute-start(bf16[32,3840]{1,0:T(8,128)(2,1)S(1)} %fusion.33), channel_id=1, source_target_pairs={{1,0},{2,1},{3,2},{4,3},{5,4},{6,5},{7,6},{9,8},{10,9},{11,10},{12... | collective-permute-start | bytes 737288 | tf_op jit(solution)/shard_map/ppermute | solution.py:94
  105.4 3.0 %collective-permute-done.11 = bf16[32,3840]{1,0:T(8,128)(2,1)S(1)} collective-permute-done((bf16[32,3840]{1,0:T(8,128)(2,1)S(1)}, bf16[32,3840]{1,0:T(8,128)(2,1)S(1)}, u32[]{:S(2)}, u32[]{:S(2)}) %collective-permute-start.11) | collective-permute-done | bytes 245792 | tf_op jit(solution)/shard_map/ppermute | solution.py:94
  109.2 0.7 fusion.31
  110.0 3.8 %collective-permute-start.12 = (bf16[32,3840]{1,0:T(8,128)(2,1)S(1)}, bf16[32,3840]{1,0:T(8,128)(2,1)S(1)}, u32[]{:S(2)}, u32[]{:S(2)}) collective-permute-start(bf16[32,3840]{1,0:T(8,128)(2,1)S(1)} %fusion.31), channel_id=1, source_target_pairs={{1,0},{2,1},{3,2},{4,3},{5,4},{6,5},{7,6},{9,8},{10,9},{11,10},{12... | collective-permute-start | bytes 737288 | tf_op jit(solution)/shard_map/ppermute | solution.py:94
  114.5 3.0 %collective-permute-done.12 = bf16[32,3840]{1,0:T(8,128)(2,1)S(1)} collective-permute-done((bf16[32,3840]{1,0:T(8,128)(2,1)S(1)}, bf16[32,3840]{1,0:T(8,128)(2,1)S(1)}, u32[]{:S(2)}, u32[]{:S(2)}) %collective-permute-start.12) | collective-permute-done | bytes 245792 | tf_op jit(solution)/shard_map/ppermute | solution.py:94
  119.0 3.8 %collective-permute-start.13 = (bf16[32,3840]{1,0:T(8,128)(2,1)S(1)}, bf16[32,3840]{1,0:T(8,128)(2,1)S(1)}, u32[]{:S(2)}, u32[]{:S(2)}) collective-permute-start(bf16[32,3840]{1,0:T(8,128)(2,1)S(1)} %fusion.29), channel_id=1, source_target_pairs={{1,0},{2,1},{3,2},{4,3},{5,4},{6,5},{7,6},{9,8},{10,9},{11,10},{12... | collective-permute-start | bytes 737288 | tf_op jit(solution)/shard_map/ppermute | solution.py:94
  123.5 3.0 %collective-permute-done.13 = bf16[32,3840]{1,0:T(8,128)(2,1)S(1)} collective-permute-done((bf16[32,3840]{1,0:T(8,128)(2,1)S(1)}, bf16[32,3840]{1,0:T(8,128)(2,1)S(1)}, u32[]{:S(2)}, u32[]{:S(2)}) %collective-permute-start.13) | collective-permute-done | bytes 245792 | tf_op jit(solution)/shard_map/ppermute | solution.py:94
  127.2 2.7 %collective-permute-start.16 = (bf16[128,512]{1,0:T(8,128)(2,1)S(1)}, bf16[128,512]{1,0:T(8,128)(2,1)S(1)}, u32[]{:S(2)}, u32[]{:S(2)}) collective-permute-start(bf16[128,512]{1,0:T(8,128)(2,1)S(1)} %pad_maximum_fusion.5), channel_id=1, source_target_pairs={{0,24},{8,0},{16,8},{24,16},{1,25},{9,1},{17,9},{25,17},{2,26},{10... | collective-permute-start | bytes 393224 | tf_op jit(solution)/shard_map/ppermute | solution.py:56
  131.1 1.3 constant_dynamic-slice_fusion.4
  132.9 2.5 %collective-permute-start.14 = (bf16[128,512]{1,0:T(8,128)(2,1)S(1)}, bf16[128,512]{1,0:T(8,128)(2,1)S(1)}, u32[]{:S(2)}, u32[]{:S(2)}) collective-permute-start(bf16[128,512]{1,0:T(8,128)(2,1)S(1)} %pad_maximum_fusion.5), channel_id=1, source_target_pairs={{0,8},{8,16},{16,24},{24,0},{1,9},{9,17},{17,25},{25,1},{2,10},{10... | collective-permute-start | bytes 393224 | tf_op jit(solution)/shard_map/ppermute | solution.py:56
  136.0 3.2 %collective-permute-start.19 = (bf16[128,960]{1,0:T(8,128)(2,1)S(1)}, bf16[128,960]{1,0:T(8,128)(2,1)S(1)}, u32[]{:S(2)}, u32[]{:S(2)}) collective-permute-start(bf16[128,960]{1,0:T(8,128)(2,1)S(1)} %get-tuple-element.99), channel_id=1, source_target_pairs={{0,24},{8,0},{16,8},{24,16},{1,25},{9,1},{17,9},{25,17},{2,26},{10... | collective-permute-start | bytes 737288 | tf_op jit(solution)/shard_map/ppermute | solution.py:47
  139.2 1.3 collective-permute-done.14
  140.6 0.9 collective-permute-start.18
  141.5 1.8 %collective-permute-start.17 = (bf16[128,960]{1,0:T(8,128)(2,1)S(1)}, bf16[128,960]{1,0:T(8,128)(2,1)S(1)}, u32[]{:S(2)}, u32[]{:S(2)}) collective-permute-start(bf16[128,960]{1,0:T(8,128)(2,1)S(1)} %get-tuple-element.101), channel_id=1, source_target_pairs={{0,8},{8,16},{16,24},{24,0},{1,9},{9,17},{17,25},{25,1},{2,10},{10... | collective-permute-start | bytes 737288 | tf_op jit(solution)/shard_map/ppermute | solution.py:47
  143.8 2.1 %collective-permute-done.19 = bf16[128,960]{1,0:T(8,128)(2,1)S(1)} collective-permute-done((bf16[128,960]{1,0:T(8,128)(2,1)S(1)}, bf16[128,960]{1,0:T(8,128)(2,1)S(1)}, u32[]{:S(2)}, u32[]{:S(2)}) %collective-permute-start.19) | collective-permute-done | bytes 245792 | tf_op jit(solution)/shard_map/ppermute | solution.py:47
  145.9 8.6 %collective-permute-done.18 = bf16[128,960]{1,0:T(8,128)(2,1)S(1)} collective-permute-done((bf16[128,960]{1,0:T(8,128)(2,1)S(1)}, bf16[128,960]{1,0:T(8,128)(2,1)S(1)}, u32[]{:S(2)}, u32[]{:S(2)}) %collective-permute-start.18) | collective-permute-done | bytes 245792 | tf_op jit(solution)/shard_map/ppermute | solution.py:47
  155.0 1.1 copy-done.4
  156.6 4.1 %fusion.27 = (bf16[1,960,512]{2,1,0:T(8,128)(2,1)}, f32[1,960,512]{2,1,0:T(8,128)}, bf16[1,960,512]{2,1,0:T(8,128)(2,1)}) fusion(f32[1,960,256]{2,1,0:T(8,128)S(1)} %convolution_bitcast_fusion, f32[1,960,256]{2,1,0:T(8,128)S(1)} %convolution_bitcast_fusion.1, bf16[1,960,512]{2,1,0:T(8,128)(2,1)S(1)} %copy-done.5, f32[1,960,512]{2,1,0:T(8,128)S(1)} %copy-done.4, ...), kind=kLoop, calls=%fused_computation.75 | loop fusion | flops 9830400 | bytes 9830400 | tf_op jit(solution)/shard_map/convert_element_type | solution.py:25
  (118 shorter events, 24.4 us)
Async XLA Ops:
  0.6 1.5 copy-start.3
  2.0 24.1 %collective-permute-start = (bf16[4,16,3840]{2,1,0:T(8,128)(2,1)S(1)}, bf16[4,16,3840]{2,1,0:T(8,128)(2,1)S(1)}, u32[]{:S(2)}, u32[]{:S(2)}) collective-permute-start(bf16[4,16,3840]{2,1,0:T(8,128)(2,1)S(1)} %get-tuple-element.103), channel_id=1, source_target_pairs={{0,7},{1,6},{2,5},{3,4},{4,3},{5,2},{6,1},{7,0},{8,15},{9,14},{10,... | collective-permute-start | bytes 1474568 | tf_op jit(solution)/shard_map/ppermute | solution.py:71
  6.1 30.5 %copy-start = (bf16[3840,512]{1,0:T(8,128)(2,1)}, bf16[3840,512]{1,0:T(8,128)(2,1)S(1)}, u32[]{:S(2)}) copy-start(bf16[3840,512]{1,0:T(8,128)(2,1)S(1)} %slice_bitcast_fusion) | copy-start | bytes 11796484
  28.8 5.7 %collective-permute-start.4 = (bf16[32,3840]{1,0:T(8,128)(2,1)S(1)}, bf16[32,3840]{1,0:T(8,128)(2,1)S(1)}, u32[]{:S(2)}, u32[]{:S(2)}) collective-permute-start(bf16[32,3840]{1,0:T(8,128)(2,1)S(1)} %fusion.2), channel_id=1, source_target_pairs={{1,0},{2,1},{3,2},{4,3},{5,4},{6,5},{7,6},{9,8},{10,9},{11,10},{12... | collective-permute-start | bytes 737288 | tf_op jit(solution)/shard_map/ppermute | solution.py:94
  38.1 7.8 %collective-permute-start.5 = (bf16[32,3840]{1,0:T(8,128)(2,1)}, bf16[32,3840]{1,0:T(8,128)(2,1)S(1)}, u32[]{:S(2)}, u32[]{:S(2)}) collective-permute-start(bf16[32,3840]{1,0:T(8,128)(2,1)} %fusion.45), channel_id=1, source_target_pairs={{1,0},{2,1},{3,2},{4,3},{5,4},{6,5},{7,6},{9,8},{10,9},{11,10},{12... | collective-permute-start | bytes 737288 | tf_op jit(solution)/shard_map/ppermute | solution.py:94
  45.9 4.2 %copy-start.1 = (bf16[3840,512]{1,0:T(8,128)(2,1)S(1)}, bf16[3840,512]{1,0:T(8,128)(2,1)}, u32[]{:S(2)}) copy-start(bf16[3840,512]{1,0:T(8,128)(2,1)} %copy-done) | copy-start | bytes 11796484
  50.8 7.4 %collective-permute-start.6 = (bf16[32,3840]{1,0:T(8,128)(2,1)S(1)}, bf16[32,3840]{1,0:T(8,128)(2,1)S(1)}, u32[]{:S(2)}, u32[]{:S(2)}) collective-permute-start(bf16[32,3840]{1,0:T(8,128)(2,1)S(1)} %fusion.43), channel_id=1, source_target_pairs={{1,0},{2,1},{3,2},{4,3},{5,4},{6,5},{7,6},{9,8},{10,9},{11,10},{12... | collective-permute-start | bytes 737288 | tf_op jit(solution)/shard_map/ppermute | solution.py:94
  61.1 8.2 %collective-permute-start.7 = (bf16[32,3840]{1,0:T(8,128)(2,1)S(1)}, bf16[32,3840]{1,0:T(8,128)(2,1)S(1)}, u32[]{:S(2)}, u32[]{:S(2)}) collective-permute-start(bf16[32,3840]{1,0:T(8,128)(2,1)S(1)} %fusion.41), channel_id=1, source_target_pairs={{1,0},{2,1},{3,2},{4,3},{5,4},{6,5},{7,6},{9,8},{10,9},{11,10},{12... | collective-permute-start | bytes 737288 | tf_op jit(solution)/shard_map/ppermute | solution.py:94
  65.0 6.6 %copy-start.7 = (bf16[11,32,256]{2,1,0:T(8,128)(2,1)S(1)}, bf16[11,32,256]{2,1,0:T(8,128)(2,1)}, u32[]{:S(2)}) copy-start(bf16[11,32,256]{2,1,0:T(8,128)(2,1)} %get-tuple-element.17) | copy-start | bytes 540676
  65.7 75.8 %collective-permute-start.3 = (bf16[128,960]{1,0:T(8,128)(2,1)S(1)}, bf16[128,960]{1,0:T(8,128)(2,1)S(1)}, u32[]{:S(2)}, u32[]{:S(2)}) collective-permute-start(bf16[128,960]{1,0:T(8,128)(2,1)S(1)} %get-tuple-element.95), channel_id=1, source_target_pairs={{0,24},{8,0},{16,8},{24,16},{1,25},{9,1},{17,9},{25,17},{2,26},{10... | collective-permute-start | bytes 737288 | tf_op jit(solution)/shard_map/ppermute | solution.py:47
  68.2 75.2 %collective-permute-start.2 = (bf16[128,960]{1,0:T(8,128)(2,1)S(1)}, bf16[128,960]{1,0:T(8,128)(2,1)S(1)}, u32[]{:S(2)}, u32[]{:S(2)}) collective-permute-start(bf16[128,960]{1,0:T(8,128)(2,1)S(1)} %get-tuple-element.96), channel_id=1, source_target_pairs={{0,16},{8,24},{16,0},{24,8},{1,17},{9,25},{17,1},{25,9},{2,18},{10... | collective-permute-start | bytes 737288 | tf_op jit(solution)/shard_map/ppermute | solution.py:47
  68.7 74.7 %collective-permute-start.1 = (bf16[128,960]{1,0:T(8,128)(2,1)S(1)}, bf16[128,960]{1,0:T(8,128)(2,1)S(1)}, u32[]{:S(2)}, u32[]{:S(2)}) collective-permute-start(bf16[128,960]{1,0:T(8,128)(2,1)S(1)} %get-tuple-element.97), channel_id=1, source_target_pairs={{0,8},{8,16},{16,24},{24,0},{1,9},{9,17},{17,25},{25,1},{2,10},{10... | collective-permute-start | bytes 737288 | tf_op jit(solution)/shard_map/ppermute | solution.py:47
  71.5 9.7 %copy-start.2 = (bf16[3840,512]{1,0:T(8,128)(2,1)S(1)}, bf16[3840,512]{1,0:T(8,128)(2,1)}, u32[]{:S(2)}) copy-start(bf16[3840,512]{1,0:T(8,128)(2,1)} %copy-done) | copy-start | bytes 11796484
  74.2 7.1 %collective-permute-start.8 = (bf16[32,3840]{1,0:T(8,128)(2,1)S(1)}, bf16[32,3840]{1,0:T(8,128)(2,1)S(1)}, u32[]{:S(2)}, u32[]{:S(2)}) collective-permute-start(bf16[32,3840]{1,0:T(8,128)(2,1)S(1)} %fusion.39), channel_id=1, source_target_pairs={{1,0},{2,1},{3,2},{4,3},{5,4},{6,5},{7,6},{9,8},{10,9},{11,10},{12... | collective-permute-start | bytes 737288 | tf_op jit(solution)/shard_map/ppermute | solution.py:94
  82.8 7.5 %collective-permute-start.9 = (bf16[32,3840]{1,0:T(8,128)(2,1)S(1)}, bf16[32,3840]{1,0:T(8,128)(2,1)S(1)}, u32[]{:S(2)}, u32[]{:S(2)}) collective-permute-start(bf16[32,3840]{1,0:T(8,128)(2,1)S(1)} %fusion.37), channel_id=1, source_target_pairs={{1,0},{2,1},{3,2},{4,3},{5,4},{6,5},{7,6},{9,8},{10,9},{11,10},{12... | collective-permute-start | bytes 737288 | tf_op jit(solution)/shard_map/ppermute | solution.py:94
  91.8 7.5 %collective-permute-start.10 = (bf16[32,3840]{1,0:T(8,128)(2,1)S(1)}, bf16[32,3840]{1,0:T(8,128)(2,1)S(1)}, u32[]{:S(2)}, u32[]{:S(2)}) collective-permute-start(bf16[32,3840]{1,0:T(8,128)(2,1)S(1)} %fusion.35), channel_id=1, source_target_pairs={{1,0},{2,1},{3,2},{4,3},{5,4},{6,5},{7,6},{9,8},{10,9},{11,10},{12... | collective-permute-start | bytes 737288 | tf_op jit(solution)/shard_map/ppermute | solution.py:94
  100.9 7.5 %collective-permute-start.11 = (bf16[32,3840]{1,0:T(8,128)(2,1)S(1)}, bf16[32,3840]{1,0:T(8,128)(2,1)S(1)}, u32[]{:S(2)}, u32[]{:S(2)}) collective-permute-start(bf16[32,3840]{1,0:T(8,128)(2,1)S(1)} %fusion.33), channel_id=1, source_target_pairs={{1,0},{2,1},{3,2},{4,3},{5,4},{6,5},{7,6},{9,8},{10,9},{11,10},{12... | collective-permute-start | bytes 737288 | tf_op jit(solution)/shard_map/ppermute | solution.py:94
  110.0 7.5 %collective-permute-start.12 = (bf16[32,3840]{1,0:T(8,128)(2,1)S(1)}, bf16[32,3840]{1,0:T(8,128)(2,1)S(1)}, u32[]{:S(2)}, u32[]{:S(2)}) collective-permute-start(bf16[32,3840]{1,0:T(8,128)(2,1)S(1)} %fusion.31), channel_id=1, source_target_pairs={{1,0},{2,1},{3,2},{4,3},{5,4},{6,5},{7,6},{9,8},{10,9},{11,10},{12... | collective-permute-start | bytes 737288 | tf_op jit(solution)/shard_map/ppermute | solution.py:94
  119.0 7.5 %collective-permute-start.13 = (bf16[32,3840]{1,0:T(8,128)(2,1)S(1)}, bf16[32,3840]{1,0:T(8,128)(2,1)S(1)}, u32[]{:S(2)}, u32[]{:S(2)}) collective-permute-start(bf16[32,3840]{1,0:T(8,128)(2,1)S(1)} %fusion.29), channel_id=1, source_target_pairs={{1,0},{2,1},{3,2},{4,3},{5,4},{6,5},{7,6},{9,8},{10,9},{11,10},{12... | collective-permute-start | bytes 737288 | tf_op jit(solution)/shard_map/ppermute | solution.py:94
  127.2 5.6 %collective-permute-start.16 = (bf16[128,512]{1,0:T(8,128)(2,1)S(1)}, bf16[128,512]{1,0:T(8,128)(2,1)S(1)}, u32[]{:S(2)}, u32[]{:S(2)}) collective-permute-start(bf16[128,512]{1,0:T(8,128)(2,1)S(1)} %pad_maximum_fusion.5), channel_id=1, source_target_pairs={{0,24},{8,0},{16,8},{24,16},{1,25},{9,1},{17,9},{25,17},{2,26},{10... | collective-permute-start | bytes 393224 | tf_op jit(solution)/shard_map/ppermute | solution.py:56
  129.9 6.1 %collective-permute-start.15 = (bf16[128,512]{1,0:T(8,128)(2,1)S(1)}, bf16[128,512]{1,0:T(8,128)(2,1)S(1)}, u32[]{:S(2)}, u32[]{:S(2)}) collective-permute-start(bf16[128,512]{1,0:T(8,128)(2,1)S(1)} %pad_maximum_fusion.5), channel_id=1, source_target_pairs={{0,16},{8,24},{16,0},{24,8},{1,17},{9,25},{17,1},{25,9},{2,18},{10... | collective-permute-start | bytes 393224 | tf_op jit(solution)/shard_map/ppermute | solution.py:56
  132.9 7.7 %collective-permute-start.14 = (bf16[128,512]{1,0:T(8,128)(2,1)S(1)}, bf16[128,512]{1,0:T(8,128)(2,1)S(1)}, u32[]{:S(2)}, u32[]{:S(2)}) collective-permute-start(bf16[128,512]{1,0:T(8,128)(2,1)S(1)} %pad_maximum_fusion.5), channel_id=1, source_target_pairs={{0,8},{8,16},{16,24},{24,0},{1,9},{9,17},{17,25},{25,1},{2,10},{10... | collective-permute-start | bytes 393224 | tf_op jit(solution)/shard_map/ppermute | solution.py:56
  136.0 9.9 %collective-permute-start.19 = (bf16[128,960]{1,0:T(8,128)(2,1)S(1)}, bf16[128,960]{1,0:T(8,128)(2,1)S(1)}, u32[]{:S(2)}, u32[]{:S(2)}) collective-permute-start(bf16[128,960]{1,0:T(8,128)(2,1)S(1)} %get-tuple-element.99), channel_id=1, source_target_pairs={{0,24},{8,0},{16,8},{24,16},{1,25},{9,1},{17,9},{25,17},{2,26},{10... | collective-permute-start | bytes 737288 | tf_op jit(solution)/shard_map/ppermute | solution.py:47
  140.6 13.9 %collective-permute-start.18 = (bf16[128,960]{1,0:T(8,128)(2,1)S(1)}, bf16[128,960]{1,0:T(8,128)(2,1)S(1)}, u32[]{:S(2)}, u32[]{:S(2)}) collective-permute-start(bf16[128,960]{1,0:T(8,128)(2,1)S(1)} %get-tuple-element.100), channel_id=1, source_target_pairs={{0,16},{8,24},{16,0},{24,8},{1,17},{9,25},{17,1},{25,9},{2,18},{10... | collective-permute-start | bytes 737288 | tf_op jit(solution)/shard_map/ppermute | solution.py:47
  141.5 13.0 %collective-permute-start.17 = (bf16[128,960]{1,0:T(8,128)(2,1)S(1)}, bf16[128,960]{1,0:T(8,128)(2,1)S(1)}, u32[]{:S(2)}, u32[]{:S(2)}) collective-permute-start(bf16[128,960]{1,0:T(8,128)(2,1)S(1)} %get-tuple-element.101), channel_id=1, source_target_pairs={{0,8},{8,16},{16,24},{24,0},{1,9},{9,17},{17,25},{25,1},{2,10},{10... | collective-permute-start | bytes 737288 | tf_op jit(solution)/shard_map/ppermute | solution.py:47
  154.5 1.5 copy-start.4
  154.5 1.8 %copy-start.5 = (bf16[1,960,512]{2,1,0:T(8,128)(2,1)S(1)}, bf16[1,960,512]{2,1,0:T(8,128)(2,1)}, u32[]{:S(2)}) copy-start(bf16[1,960,512]{2,1,0:T(8,128)(2,1)} %param.9) | copy-start | bytes 2949124
  154.5 2.1 %copy-start.6 = (bf16[1,960,512]{2,1,0:T(8,128)(2,1)S(1)}, bf16[1,960,512]{2,1,0:T(8,128)(2,1)}, u32[]{:S(2)}) copy-start(bf16[1,960,512]{2,1,0:T(8,128)(2,1)} %param.8) | copy-start | bytes 2949124

commit v2 on v1

v2 whole, which is shorter than its diff:
```python
import functools

import jax
import jax.numpy as jnp
from jax import lax
from jax.experimental import pallas as pl
from jax.experimental.pallas import tpu as pltpu
from jax.sharding import PartitionSpec as P

norm_epsilon = 1e-06
first_decay = 0.9
second_decay = 0.95
adam_epsilon = 1e-08
learn_rate = 0.00022
weight_decay = 0.1
step_count = 100.0


def adamw(master, moment1, moment2, gradient):
    first_new = first_decay * moment1.astype(jnp.float32) + (1.0 - first_decay) * gradient
    second_new = (
        second_decay * moment2.astype(jnp.float32) + (1.0 - second_decay) * gradient * gradient
    )
    first_hat = first_new / (1.0 - first_decay**step_count)
    second_hat = second_new / (1.0 - second_decay**step_count)
    updated = master - learn_rate * (
        first_hat / (jnp.sqrt(second_hat) + adam_epsilon) + weight_decay * master
    )
    return (updated, first_new.astype(jnp.bfloat16), second_new.astype(jnp.bfloat16))


def chain_kernel(
    n_dp, sections, weights_ref, saved_ref, cot_ref,
    normed_all, wide_all, narrow_all,
    w, arrived, outgoing, swapped, normed_cut, wide_cut, latents, scales,
    w_sem, ex_send, ex_recv, chain_send, chain_recv, swap_send, swap_recv,
):
    me = lax.axis_index("dp")
    position = lax.axis_index("pipe")
    pieces, rows, features = saved_ref.shape
    half = pieces // 2
    rank = w.shape[1] // 2
    cut = features // n_dp
    partner = sections - 1 - position
    below = lax.rem(position + sections - 1, sections)
    above = lax.rem(position + 1, sections)

    w_copy = pltpu.make_async_copy(weights_ref.at[0], w, w_sem)
    w_copy.start()

    barrier = pltpu.get_barrier_semaphore()

    def greet(device):
        pl.semaphore_signal(
            barrier, inc=1, device_id=device, device_id_type=pl.DeviceIdType.MESH
        )

    for apart in range(1, n_dp):
        greet({"dp": lax.rem(me + apart, n_dp)})
    for device in (partner, below, above):
        greet({"pipe": device})
    pl.semaphore_wait(barrier, n_dp + 2)

    def remote(source, target, send, receive, device):
        return pltpu.make_async_remote_copy(
            src_ref=source, dst_ref=target, send_sem=send, recv_sem=receive,
            device_id=device, device_id_type=pl.DeviceIdType.MESH,
        )

    def swap_copy(h):
        return remote(
            saved_ref.at[half + h], swapped.at[h], swap_send.at[h], swap_recv.at[h],
            {"pipe": partner},
        )

    def chain_copy(k):
        return remote(
            outgoing.at[k], arrived.at[k], chain_send.at[k], chain_recv.at[k], {"pipe": below}
        )

    def exchange(kind, apart, k):
        peer = lax.rem(me + apart, n_dp)
        target = (normed_all, wide_all, narrow_all)[kind]
        source = (
            normed_cut.at[peer, k], wide_cut.at[peer, k], narrow_all.at[0, k]
        )[kind]
        return remote(
            source, target.at[apart, k], ex_send.at[kind, apart, k],
            ex_recv.at[kind, apart, k], {"dp": peer},
        )

    for h in range(half):
        swap_copy(h).start()
    w_copy.wait()

    def prepare(k):
        if k < half:
            x = saved_ref[k]
        else:
            swap_copy(k - half).wait_recv()
            x = swapped[k - half]
        values = x.astype(jnp.float32)
        row_scale = lax.rsqrt(jnp.mean(values * values, axis=-1, keepdims=True) + norm_epsilon)
        normed = (values * row_scale).astype(jnp.bfloat16)
        latent = jnp.dot(normed, w[:, :rank], preferred_element_type=jnp.float32)
        latents[k] = latent
        scales[k] = jnp.broadcast_to(row_scale, scales.shape[1:])
        latent_scale = lax.rsqrt(jnp.mean(latent * latent, axis=-1, keepdims=True) + norm_epsilon)
        narrow_all[0, k, :, rank:] = (latent * latent_scale).astype(jnp.bfloat16)
        for owner in range(n_dp):
            normed_cut[owner, k] = normed[:, owner * cut : (owner + 1) * cut]
        for apart in range(1, n_dp):
            exchange(0, apart, k).start()
        normed_all[0, k] = normed_cut[me, k]

    def advance(k):
        @pl.when(position == sections - 1)
        def _():
            arrived[k] = cot_ref[k]

        @pl.when(position < sections - 1)
        def _():
            chain_copy(k).wait_recv()

        grad_out = arrived[k]
        latent = latents[k]
        row_scale = scales[k][:, :1]
        latent_scale = lax.rsqrt(jnp.mean(latent * latent, axis=-1, keepdims=True) + norm_epsilon)
        grad_act = jnp.dot(grad_out, w[:, rank:], preferred_element_type=jnp.float32)
        grad_latent = latent_scale * grad_act - latent * latent_scale**3 * jnp.mean(
            latent * grad_act, axis=-1, keepdims=True
        )
        grad_latent = grad_latent.astype(jnp.bfloat16)
        narrow_all[0, k, :, :rank] = grad_latent

        @pl.when(position > 0)
        def _():
            along = jnp.sum(latent * grad_latent.astype(jnp.float32), axis=-1, keepdims=True)
            along = along * (row_scale * row_scale / features)
            x = saved_ref[k] if k < half else swapped[k - half]
            grad_normed = lax.dot_general(
                grad_latent, w[:, :rank], (((1,), (1,)), ((), ())),
                preferred_element_type=jnp.float32,
            )
            outgoing[k] = (
                arrived[k].astype(jnp.float32)
                + row_scale * grad_normed
                - x.astype(jnp.float32) * along
            ).astype(jnp.bfloat16)
            chain_copy(k).start()

        for owner in range(n_dp):
            wide_cut[owner, k] = arrived[k, :, owner * cut : (owner + 1) * cut]
        for apart in range(1, n_dp):
            exchange(1, apart, k).start()
            exchange(2, apart, k).start()
        wide_all[0, k] = wide_cut[me, k]

    for k in range(half):
        prepare(k)
    for k in range(half):
        advance(k)
    for k in range(half, pieces):
        prepare(k)
        advance(k)

    for h in range(half):
        swap_copy(h).wait_send()

    @pl.when(position > 0)
    def _():
        for k in range(pieces):
            chain_copy(k).wait_send()

    for kind in range(3):
        for apart in range(1, n_dp):
            for k in range(pieces):
                exchange(kind, apart, k).wait()


def shards(weights, master, moment1, moment2, saved, cotangent):
    n_dp = lax.axis_size("dp")
    sections = lax.axis_size("pipe")
    micro, batch_rows, features = saved.shape[2:]
    width = weights.shape[3]
    rank = width // 2
    pieces = micro
    rows = 2 * micro * batch_rows // pieces
    cut = features // n_dp
    bf16, f32 = jnp.bfloat16, jnp.float32
    vmem = pl.BlockSpec(memory_space=pltpu.VMEM)
    flops = 2 * pieces * rows * features * rank * 3
    normed_all, wide_all, narrow_all = pl.pallas_call(
        functools.partial(chain_kernel, n_dp, sections),
        out_shape=[
            jax.ShapeDtypeStruct((n_dp, pieces, rows, cut), bf16),
            jax.ShapeDtypeStruct((n_dp, pieces, rows, cut), bf16),
            jax.ShapeDtypeStruct((n_dp, pieces, rows, width), bf16),
        ],
        in_specs=[pl.BlockSpec(memory_space=pl.ANY), vmem, vmem],
        out_specs=[vmem, vmem, vmem],
        scratch_shapes=[
            pltpu.VMEM((features, width), bf16),
            pltpu.VMEM((pieces, rows, features), bf16),
            pltpu.VMEM((pieces, rows, features), bf16),
            pltpu.VMEM((pieces // 2, rows, features), bf16),
            pltpu.VMEM((n_dp, pieces, rows, cut), bf16),
            pltpu.VMEM((n_dp, pieces, rows, cut), bf16),
            pltpu.VMEM((pieces, rows, rank), f32),
            pltpu.VMEM((pieces, rows, 128), f32),
            pltpu.SemaphoreType.DMA,
            pltpu.SemaphoreType.DMA((3, n_dp, pieces)),
            pltpu.SemaphoreType.DMA((3, n_dp, pieces)),
            pltpu.SemaphoreType.DMA((pieces,)),
            pltpu.SemaphoreType.DMA((pieces,)),
            pltpu.SemaphoreType.DMA((pieces // 2,)),
            pltpu.SemaphoreType.DMA((pieces // 2,)),
        ],
        compiler_params=pltpu.CompilerParams(
            collective_id=0, has_side_effects=True, vmem_limit_bytes=44 * 2**20
        ),
        cost_estimate=pl.CostEstimate(
            flops=flops, bytes_accessed=features * width * 2, transcendentals=0
        ),
    )(
        weights.reshape(2, features, width),
        saved.reshape(pieces, rows, features),
        cotangent.reshape(pieces, rows, features),
    )
    normed_all = normed_all.reshape(-1, cut)
    wide_all = wide_all.reshape(-1, cut)
    narrow_all = narrow_all.reshape(-1, width)
    down_part = jnp.einsum("td,tk->dk", normed_all, narrow_all[:, :rank], preferred_element_type=f32)
    up_part = jnp.einsum("td,tk->dk", wide_all, narrow_all[:, rank:], preferred_element_type=f32)
    gradient = jnp.concatenate([down_part, up_part], axis=1)
    new_master, new_first, new_second = adamw(master[0], moment1[0], moment2[0], gradient)
    return (new_master[None], new_first[None], new_second[None])


def solution(mesh):
    return jax.shard_map(
        shards,
        mesh=mesh,
        in_specs=(
            P("pipe", None, None, None),
            P("pipe", "dp", None),
            P("pipe", "dp", None),
            P("pipe", "dp", None),
            P("pipe", None, None, "dp", None),
            P(None, None, "dp", None),
        ),
        out_specs=(P("pipe", "dp", None), P("pipe", "dp", None), P("pipe", "dp", None)),
        check_vma=False,
    )
```

time: 161 us -> 75.8 us (0.47)
  the two profiles are of different devices: /device:TPU:16 before, /device:TPU:0 now
where the time goes in v2:
time: 75.8 us; the launch traced here: 75.6 us
  Pallas kernels  66.4 us (88%)
  other arithmetic  4.08 us (5%)
  local copies, waits for them, and re-layouts  3.53 us (5%)
  matrix products  0.92 us (1%)
    pallas_call x1, Pallas kernels, shards(): pl.pallas_call(functools.partial(chain_kernel, n_dp, sections), out_shape...  66.4 us
    convert_element_type x1, other arithmetic, adamw(): second_new.astype(jnp.bfloat16)  4.08 us
    unnamed x10, local copies, waits for them, and re-layouts  3.53 us

profile of v2, /device:TPU:0, one launch (start us, length us, event | category | flops | bytes accessed | tf_op | source)
XLA Modules:
  0.0 75.6 jit_solution(114275256787654259)
XLA Ops:
  0.6 0.0 copy-start
  0.6 1.2 %copy-done = bf16[1,2,4,16,3840]{4,3,2,1,0:T(8,128)(2,1)S(1)} copy-done((bf16[1,2,4,16,3840]{4,3,2,1,0:T(8,128)(2,1)S(1)}, bf16[1,2,4,16,3840]{4,3,2,1,0:T(8,128)(2,1)}, u32[]{:S(2)}) %copy-start) | copy-done | bytes 983064
  1.8 0.0 copy-start.1
  1.8 1.2 %copy-done.1 = bf16[2,4,16,3840]{3,2,1,0:T(8,128)(2,1)S(1)} copy-done((bf16[2,4,16,3840]{3,2,1,0:T(8,128)(2,1)S(1)}, bf16[2,4,16,3840]{3,2,1,0:T(8,128)(2,1)}, u32[]{:S(2)}) %copy-start.1) | copy-done | bytes 983064
  3.0 66.4 %shard_map.85 = (bf16[4,4,32,960]{3,2,1,0:T(8,128)(2,1)S(1)}, bf16[4,4,32,960]{3,2,1,0:T(8,128)(2,1)S(1)}, bf16[4,4,32,512]{3,2,1,0:T(8,128)(2,1)S(1)}) custom-call(bf16[2,3840,512]{2,1,0:T(8,128)(2,1)} %bitcast.18, bf16[4,32,3840]{2,1,0:T(8,128)(2,1)S(1)} %bitcast.14, bf16[4,32,3840]{2,1,0:T(8,128)(2,1)S(1)} %bitcast.15), custom_call_target="tpu_custom_call" | custom-call | flops 754974720 | bytes 3932160 | tf_op jit(solution)/shard_map/pallas_call | solution.py:193
  69.4 0.0 copy-start.2
  69.4 0.0 copy-start.3
  69.4 0.0 copy-start.4
  69.4 0.5 convolution_bitcast_fusion
  69.9 0.5 convolution_bitcast_fusion.1
  70.4 0.6 copy-done.2
  71.0 0.2 copy-done.3
  71.2 0.3 copy-done.4
  71.5 4.1 %fusion.2 = (bf16[1,960,512]{2,1,0:T(8,128)(2,1)}, f32[1,960,512]{2,1,0:T(8,128)}, bf16[1,960,512]{2,1,0:T(8,128)(2,1)}) fusion(f32[1,960,256]{2,1,0:T(8,128)S(1)} %convolution_bitcast_fusion, f32[1,960,256]{2,1,0:T(8,128)S(1)} %convolution_bitcast_fusion.1, bf16[1,960,512]{2,1,0:T(8,128)(2,1)S(1)} %copy-done.3, f32[1,960,512]{2,1,0:T(8,128)S(1)} %copy-done.2, ...), kind=kLoop, calls=%fused_computation.8 | loop fusion | flops 9830400 | bytes 9830400 | tf_op jit(solution)/shard_map/convert_element_type | solution.py:29
Async XLA Ops:
  0.6 1.2 %copy-start = (bf16[1,2,4,16,3840]{4,3,2,1,0:T(8,128)(2,1)S(1)}, bf16[1,2,4,16,3840]{4,3,2,1,0:T(8,128)(2,1)}, u32[]{:S(2)}) copy-start(bf16[1,2,4,16,3840]{4,3,2,1,0:T(8,128)(2,1)} %param.10) | copy-start | bytes 2949124
  1.8 1.2 %copy-start.1 = (bf16[2,4,16,3840]{3,2,1,0:T(8,128)(2,1)S(1)}, bf16[2,4,16,3840]{3,2,1,0:T(8,128)(2,1)}, u32[]{:S(2)}) copy-start(bf16[2,4,16,3840]{3,2,1,0:T(8,128)(2,1)} %param.11) | copy-start | bytes 2949124
  69.4 1.5 %copy-start.2 = (f32[1,960,512]{2,1,0:T(8,128)S(1)}, f32[1,960,512]{2,1,0:T(8,128)}, u32[]{:S(2)}) copy-start(f32[1,960,512]{2,1,0:T(8,128)} %param.7) | copy-start | bytes 5898244
  69.4 1.8 %copy-start.3 = (bf16[1,960,512]{2,1,0:T(8,128)(2,1)S(1)}, bf16[1,960,512]{2,1,0:T(8,128)(2,1)}, u32[]{:S(2)}) copy-start(bf16[1,960,512]{2,1,0:T(8,128)(2,1)} %param.9) | copy-start | bytes 2949124
  69.4 2.1 %copy-start.4 = (bf16[1,960,512]{2,1,0:T(8,128)(2,1)S(1)}, bf16[1,960,512]{2,1,0:T(8,128)(2,1)}, u32[]{:S(2)}) copy-start(bf16[1,960,512]{2,1,0:T(8,128)(2,1)} %param.8) | copy-start | bytes 2949124

commit v3 on v2

--- a/solution.py
+++ b/solution.py
@@ -32,8 +32,9 @@
 def chain_kernel(
     n_dp, sections, weights_ref, saved_ref, cot_ref,
     normed_all, wide_all, narrow_all,
-    w, arrived, outgoing, swapped, normed_cut, wide_cut, latents, scales,
-    w_sem, ex_send, ex_recv, chain_send, chain_recv, swap_send, swap_recv,
+    w, here, arrived, outgoing, swapped, normed_cut, wide_cut, latents, scales,
+    w_sem, here_sem, cot_sem, ex_send, ex_recv, chain_send, chain_recv, swap_send, swap_recv,
+    turn,
 ):
     me = lax.axis_index("dp")
     position = lax.axis_index("pipe")
@@ -41,12 +42,24 @@
     half = pieces // 2
     rank = w.shape[1] // 2
     cut = features // n_dp
+    chunks = chain_send.shape[1]
+    chunk = features // chunks
+    columns = [pl.ds(c * chunk, chunk) for c in range(chunks)]
+    lower = sections // 2
+    late = lower + sections // 4
     partner = sections - 1 - position
     below = lax.rem(position + sections - 1, sections)
     above = lax.rem(position + 1, sections)
 
     w_copy = pltpu.make_async_copy(weights_ref.at[0], w, w_sem)
     w_copy.start()
+    here_copy = pltpu.make_async_copy(saved_ref.at[pl.ds(0, half)], here, here_sem)
+    here_copy.start()
+    cot_copy = pltpu.make_async_copy(cot_ref, arrived, cot_sem)
+
+    @pl.when(position == sections - 1)
+    def _():
+        cot_copy.start()
 
     barrier = pltpu.get_barrier_semaphore()
 
@@ -67,15 +80,21 @@
             device_id=device, device_id_type=pl.DeviceIdType.MESH,
         )
 
-    def swap_copy(h):
+    def swap_copy(h, c):
         return remote(
-            saved_ref.at[half + h], swapped.at[h], swap_send.at[h], swap_recv.at[h],
-            {"pipe": partner},
-        )
-
-    def chain_copy(k):
+            saved_ref.at[half + h, :, columns[c]], swapped.at[h, :, columns[c]],
+            swap_send.at[h, c], swap_recv.at[h, c], {"pipe": partner},
+        )
+
+    def swap_each(act):
+        for h in range(half):
+            for c in range(chunks):
+                act(swap_copy(h, c))
+
+    def chain_copy(k, c):
         return remote(
-            outgoing.at[k], arrived.at[k], chain_send.at[k], chain_recv.at[k], {"pipe": below}
+            outgoing.at[k, :, columns[c]], arrived.at[k, :, columns[c]],
+            chain_send.at[k, c], chain_recv.at[k, c], {"pipe": below},
         )
 
     def exchange(kind, apart, k):
@@ -89,15 +108,19 @@
             ex_recv.at[kind, apart, k], {"dp": peer},
         )
 
-    for h in range(half):
-        swap_copy(h).start()
+    @pl.when((position == 0) | ((position >= lower) & (position < late)))
+    def _():
+        swap_each(lambda copy: copy.start())
+
+    here_copy.wait()
     w_copy.wait()
 
     def prepare(k):
         if k < half:
-            x = saved_ref[k]
+            x = here[k]
         else:
-            swap_copy(k - half).wait_recv()
+            for c in range(chunks):
+                swap_copy(k - half, c).wait_recv()
             x = swapped[k - half]
         values = x.astype(jnp.float32)
         row_scale = lax.rsqrt(jnp.mean(values * values, axis=-1, keepdims=True) + norm_epsilon)
@@ -116,17 +139,23 @@
     def advance(k):
         @pl.when(position == sections - 1)
         def _():
-            arrived[k] = cot_ref[k]
-
-        @pl.when(position < sections - 1)
-        def _():
-            chain_copy(k).wait_recv()
-
-        grad_out = arrived[k]
+            if k == 0:
+                cot_copy.wait()
+
         latent = latents[k]
         row_scale = scales[k][:, :1]
         latent_scale = lax.rsqrt(jnp.mean(latent * latent, axis=-1, keepdims=True) + norm_epsilon)
-        grad_act = jnp.dot(grad_out, w[:, rank:], preferred_element_type=jnp.float32)
+        grad_act = jnp.zeros((rows, rank), jnp.float32)
+        for c in range(chunks):
+
+            @pl.when(position < sections - 1)
+            def _():
+                chain_copy(k, c).wait_recv()
+
+            grad_act += jnp.dot(
+                arrived[k, :, columns[c]], w[columns[c], rank:],
+                preferred_element_type=jnp.float32,
+            )
         grad_latent = latent_scale * grad_act - latent * latent_scale**3 * jnp.mean(
             latent * grad_act, axis=-1, keepdims=True
         )
@@ -137,17 +166,18 @@
         def _():
             along = jnp.sum(latent * grad_latent.astype(jnp.float32), axis=-1, keepdims=True)
             along = along * (row_scale * row_scale / features)
-            x = saved_ref[k] if k < half else swapped[k - half]
-            grad_normed = lax.dot_general(
-                grad_latent, w[:, :rank], (((1,), (1,)), ((), ())),
-                preferred_element_type=jnp.float32,
-            )
-            outgoing[k] = (
-                arrived[k].astype(jnp.float32)
-                + row_scale * grad_normed
-                - x.astype(jnp.float32) * along
-            ).astype(jnp.bfloat16)
-            chain_copy(k).start()
+            x_ref = here.at[k] if k < half else swapped.at[k - half]
+            for c in range(chunks):
+                grad_normed = lax.dot_general(
+                    grad_latent, w[columns[c], :rank], (((1,), (1,)), ((), ())),
+                    preferred_element_type=jnp.float32,
+                )
+                outgoing[k, :, columns[c]] = (
+                    arrived[k, :, columns[c]].astype(jnp.float32)
+                    + row_scale * grad_normed
+                    - x_ref[:, columns[c]].astype(jnp.float32) * along
+                ).astype(jnp.bfloat16)
+                chain_copy(k, c).start()
 
         for owner in range(n_dp):
             wide_cut[owner, k] = arrived[k, :, owner * cut : (owner + 1) * cut]
@@ -158,19 +188,38 @@
 
     for k in range(half):
         prepare(k)
+
+    @pl.when((position > 0) & (position < lower))
+    def _():
+        pl.semaphore_wait(turn, 1)
+        swap_each(lambda copy: copy.start())
+
+    @pl.when(position < lower - 1)
+    def _():
+        swap_each(lambda copy: copy.wait_send())
+        pl.semaphore_signal(
+            turn, inc=1, device_id={"pipe": above}, device_id_type=pl.DeviceIdType.MESH
+        )
+
     for k in range(half):
         advance(k)
     for k in range(half, pieces):
         prepare(k)
         advance(k)
 
-    for h in range(half):
-        swap_copy(h).wait_send()
+    @pl.when(position >= late)
+    def _():
+        swap_each(lambda copy: copy.start())
+
+    @pl.when(position >= lower - 1)
+    def _():
+        swap_each(lambda copy: copy.wait_send())
 
     @pl.when(position > 0)
     def _():
         for k in range(pieces):
-            chain_copy(k).wait_send()
+            for c in range(chunks):
+                chain_copy(k, c).wait_send()
 
     for kind in range(3):
         for apart in range(1, n_dp):
@@ -187,6 +236,7 @@
     pieces = micro
     rows = 2 * micro * batch_rows // pieces
     cut = features // n_dp
+    chunks = 5 if features % (5 * 128) == 0 else 1
     bf16, f32 = jnp.bfloat16, jnp.float32
     vmem = pl.BlockSpec(memory_space=pltpu.VMEM)
     flops = 2 * pieces * rows * features * rank * 3
@@ -197,10 +247,11 @@
             jax.ShapeDtypeStruct((n_dp, pieces, rows, cut), bf16),
             jax.ShapeDtypeStruct((n_dp, pieces, rows, width), bf16),
         ],
-        in_specs=[pl.BlockSpec(memory_space=pl.ANY), vmem, vmem],
+        in_specs=[pl.BlockSpec(memory_space=pl.ANY)] * 3,
         out_specs=[vmem, vmem, vmem],
         scratch_shapes=[
             pltpu.VMEM((features, width), bf16),
+            pltpu.VMEM((pieces // 2, rows, features), bf16),
             pltpu.VMEM((pieces, rows, features), bf16),
             pltpu.VMEM((pieces, rows, features), bf16),
             pltpu.VMEM((pieces // 2, rows, features), bf16),
@@ -209,12 +260,15 @@
             pltpu.VMEM((pieces, rows, rank), f32),
             pltpu.VMEM((pieces, rows, 128), f32),
             pltpu.SemaphoreType.DMA,
+            pltpu.SemaphoreType.DMA,
+            pltpu.SemaphoreType.DMA,
             pltpu.SemaphoreType.DMA((3, n_dp, pieces)),
             pltpu.SemaphoreType.DMA((3, n_dp, pieces)),
-            pltpu.SemaphoreType.DMA((pieces,)),
-            pltpu.SemaphoreType.DMA((pieces,)),
-            pltpu.SemaphoreType.DMA((pieces // 2,)),
-            pltpu.SemaphoreType.DMA((pieces // 2,)),
+            pltpu.SemaphoreType.DMA((pieces, chunks)),
+            pltpu.SemaphoreType.DMA((pieces, chunks)),
+            pltpu.SemaphoreType.DMA((pieces // 2, chunks)),
+            pltpu.SemaphoreType.DMA((pieces // 2, chunks)),
+            pltpu.SemaphoreType.REGULAR,
         ],
         compiler_params=pltpu.CompilerParams(
             collective_id=0, has_side_effects=True, vmem_limit_bytes=44 * 2**20

time: 75.8 us -> 76.3 us (level)
  no operation moved by 1% of the time
where the time goes in v3:
time: 76.3 us; the launch traced here: 76.1 us
  Pallas kernels  66.9 us (88%)
  other arithmetic  4.08 us (5%)
  local copies, waits for them, and re-layouts  3.53 us (5%)
  matrix products  0.92 us (1%)
    pallas_call x1, Pallas kernels, shards(): pl.pallas_call(functools.partial(chain_kernel, n_dp, sections), out_shape...  66.9 us
    convert_element_type x1, other arithmetic, adamw(): second_new.astype(jnp.bfloat16)  4.08 us
    unnamed x10, local copies, waits for them, and re-layouts  3.53 us

profile of v3, /device:TPU:0, one launch (start us, length us, event | category | flops | bytes accessed | tf_op | source)
XLA Modules:
  0.0 76.1 jit_solution(15048628049795054847)
XLA Ops:
  0.6 0.0 copy-start
  0.6 1.2 %copy-done = bf16[1,2,4,16,3840]{4,3,2,1,0:T(8,128)(2,1)S(1)} copy-done((bf16[1,2,4,16,3840]{4,3,2,1,0:T(8,128)(2,1)S(1)}, bf16[1,2,4,16,3840]{4,3,2,1,0:T(8,128)(2,1)}, u32[]{:S(2)}) %copy-start) | copy-done | bytes 983064
  1.8 0.0 copy-start.1
  1.8 1.2 %copy-done.1 = bf16[2,4,16,3840]{3,2,1,0:T(8,128)(2,1)S(1)} copy-done((bf16[2,4,16,3840]{3,2,1,0:T(8,128)(2,1)S(1)}, bf16[2,4,16,3840]{3,2,1,0:T(8,128)(2,1)}, u32[]{:S(2)}) %copy-start.1) | copy-done | bytes 983064
  3.0 66.9 %shard_map.85 = (bf16[4,4,32,960]{3,2,1,0:T(8,128)(2,1)S(1)}, bf16[4,4,32,960]{3,2,1,0:T(8,128)(2,1)S(1)}, bf16[4,4,32,512]{3,2,1,0:T(8,128)(2,1)S(1)}) custom-call(bf16[2,3840,512]{2,1,0:T(8,128)(2,1)} %bitcast.18, bf16[4,32,3840]{2,1,0:T(8,128)(2,1)S(1)} %bitcast.14, bf16[4,32,3840]{2,1,0:T(8,128)(2,1)S(1)} %bitcast.15), custom_call_target="tpu_custom_call" | custom-call | flops 754974720 | bytes 3932160 | tf_op jit(solution)/shard_map/pallas_call | solution.py:243
  69.9 0.0 copy-start.2
  69.9 0.0 copy-start.3
  69.9 0.0 copy-start.4
  69.9 0.5 convolution_bitcast_fusion
  70.4 0.5 convolution_bitcast_fusion.1
  70.9 0.6 copy-done.2
  71.5 0.2 copy-done.3
  71.7 0.3 copy-done.4
  72.0 4.1 %fusion.2 = (bf16[1,960,512]{2,1,0:T(8,128)(2,1)}, f32[1,960,512]{2,1,0:T(8,128)}, bf16[1,960,512]{2,1,0:T(8,128)(2,1)}) fusion(f32[1,960,256]{2,1,0:T(8,128)S(1)} %convolution_bitcast_fusion, f32[1,960,256]{2,1,0:T(8,128)S(1)} %convolution_bitcast_fusion.1, bf16[1,960,512]{2,1,0:T(8,128)(2,1)S(1)} %copy-done.3, f32[1,960,512]{2,1,0:T(8,128)S(1)} %copy-done.2, ...), kind=kLoop, calls=%fused_computation.8 | loop fusion | flops 9830400 | bytes 9830400 | tf_op jit(solution)/shard_map/convert_element_type | solution.py:29
Async XLA Ops:
  0.6 1.2 %copy-start = (bf16[1,2,4,16,3840]{4,3,2,1,0:T(8,128)(2,1)S(1)}, bf16[1,2,4,16,3840]{4,3,2,1,0:T(8,128)(2,1)}, u32[]{:S(2)}) copy-start(bf16[1,2,4,16,3840]{4,3,2,1,0:T(8,128)(2,1)} %param.10) | copy-start | bytes 2949124
  1.8 1.2 %copy-start.1 = (bf16[2,4,16,3840]{3,2,1,0:T(8,128)(2,1)S(1)}, bf16[2,4,16,3840]{3,2,1,0:T(8,128)(2,1)}, u32[]{:S(2)}) copy-start(bf16[2,4,16,3840]{3,2,1,0:T(8,128)(2,1)} %param.11) | copy-start | bytes 2949124
  69.9 1.5 %copy-start.2 = (f32[1,960,512]{2,1,0:T(8,128)S(1)}, f32[1,960,512]{2,1,0:T(8,128)}, u32[]{:S(2)}) copy-start(f32[1,960,512]{2,1,0:T(8,128)} %param.7) | copy-start | bytes 5898244
  69.9 1.8 %copy-start.3 = (bf16[1,960,512]{2,1,0:T(8,128)(2,1)S(1)}, bf16[1,960,512]{2,1,0:T(8,128)(2,1)}, u32[]{:S(2)}) copy-start(bf16[1,960,512]{2,1,0:T(8,128)(2,1)} %param.9) | copy-start | bytes 2949124
  69.9 2.1 %copy-start.4 = (bf16[1,960,512]{2,1,0:T(8,128)(2,1)S(1)}, bf16[1,960,512]{2,1,0:T(8,128)(2,1)}, u32[]{:S(2)}) copy-start(bf16[1,960,512]{2,1,0:T(8,128)(2,1)} %param.8) | copy-start | bytes 2949124

commit v4 on v3

--- a/solution.py
+++ b/solution.py
@@ -186,8 +186,7 @@
             exchange(2, apart, k).start()
         wide_all[0, k] = wide_cut[me, k]
 
-    for k in range(half):
-        prepare(k)
+    prepare(0)
 
     @pl.when((position > 0) & (position < lower))
     def _():
@@ -201,11 +200,10 @@
             turn, inc=1, device_id={"pipe": above}, device_id_type=pl.DeviceIdType.MESH
         )
 
-    for k in range(half):
+    for k in range(pieces):
         advance(k)
-    for k in range(half, pieces):
-        prepare(k)
-        advance(k)
+        if k + 1 < pieces:
+            prepare(k + 1)
 
     @pl.when(position >= late)
     def _():
@@ -233,10 +231,10 @@
     micro, batch_rows, features = saved.shape[2:]
     width = weights.shape[3]
     rank = width // 2
-    pieces = micro
+    pieces = 2 * micro
     rows = 2 * micro * batch_rows // pieces
     cut = features // n_dp
-    chunks = 5 if features % (5 * 128) == 0 else 1
+    chunks = 3 if features % (3 * 128) == 0 else 1
     bf16, f32 = jnp.bfloat16, jnp.float32
     vmem = pl.BlockSpec(memory_space=pltpu.VMEM)
     flops = 2 * pieces * rows * features * rank * 3

time: 76.3 us -> 82.7 us (1.084)
  Pallas kernels: 66.9 us -> 73.2 us
    pallas_call x1, Pallas kernels: 66.9 us -> 73.2 us  [shards(): pl.pallas_call(functools.partial(chain_kernel, n_dp, sections), out_shape...]
where the time goes in v4:
time: 82.7 us; the launch traced here: 82.5 us
  Pallas kernels  73.2 us (89%)
  other arithmetic  4.08 us (5%)
  local copies, waits for them, and re-layouts  3.53 us (4%)
  matrix products  0.92 us (1%)
    pallas_call x1, Pallas kernels, shards(): pl.pallas_call(functools.partial(chain_kernel, n_dp, sections), out_shape...  73.2 us
    convert_element_type x1, other arithmetic, adamw(): second_new.astype(jnp.bfloat16)  4.08 us
    unnamed x10, local copies, waits for them, and re-layouts  3.53 us

profile of v4, /device:TPU:0, one launch (start us, length us, event | category | flops | bytes accessed | tf_op | source)
XLA Modules:
  0.0 82.5 jit_solution(3738393996546562062)
XLA Ops:
  0.6 0.0 copy-start
  0.6 1.2 %copy-done = bf16[1,2,4,16,3840]{4,3,2,1,0:T(8,128)(2,1)S(1)} copy-done((bf16[1,2,4,16,3840]{4,3,2,1,0:T(8,128)(2,1)S(1)}, bf16[1,2,4,16,3840]{4,3,2,1,0:T(8,128)(2,1)}, u32[]{:S(2)}) %copy-start) | copy-done | bytes 983064
  1.8 0.0 copy-start.1
  1.8 1.2 %copy-done.1 = bf16[2,4,16,3840]{3,2,1,0:T(8,128)(2,1)S(1)} copy-done((bf16[2,4,16,3840]{3,2,1,0:T(8,128)(2,1)S(1)}, bf16[2,4,16,3840]{3,2,1,0:T(8,128)(2,1)}, u32[]{:S(2)}) %copy-start.1) | copy-done | bytes 983064
  3.0 73.2 %shard_map.85 = (bf16[4,8,16,960]{3,2,1,0:T(8,128)(2,1)S(1)}, bf16[4,8,16,960]{3,2,1,0:T(8,128)(2,1)S(1)}, bf16[4,8,16,512]{3,2,1,0:T(8,128)(2,1)S(1)}) custom-call(bf16[2,3840,512]{2,1,0:T(8,128)(2,1)} %bitcast.18, bf16[8,16,3840]{2,1,0:T(8,128)(2,1)S(1)} %bitcast.14, bf16[8,16,3840]{2,1,0:T(8,128)(2,1)S(1)} %bitcast.15), custom_call_target="tpu_custom_call" | custom-call | flops 754974720 | bytes 3932160 | tf_op jit(solution)/shard_map/pallas_call | solution.py:241
  76.3 0.0 copy-start.2
  76.3 0.0 copy-start.3
  76.3 0.0 copy-start.4
  76.3 0.5 convolution_bitcast_fusion
  76.8 0.5 convolution_bitcast_fusion.1
  77.3 0.6 copy-done.2
  77.8 0.2 copy-done.3
  78.1 0.3 copy-done.4
  78.4 4.1 %fusion.2 = (bf16[1,960,512]{2,1,0:T(8,128)(2,1)}, f32[1,960,512]{2,1,0:T(8,128)}, bf16[1,960,512]{2,1,0:T(8,128)(2,1)}) fusion(f32[1,960,256]{2,1,0:T(8,128)S(1)} %convolution_bitcast_fusion, f32[1,960,256]{2,1,0:T(8,128)S(1)} %convolution_bitcast_fusion.1, bf16[1,960,512]{2,1,0:T(8,128)(2,1)S(1)} %copy-done.3, f32[1,960,512]{2,1,0:T(8,128)S(1)} %copy-done.2, ...), kind=kLoop, calls=%fused_computation.8 | loop fusion | flops 9830400 | bytes 9830400 | tf_op jit(solution)/shard_map/convert_element_type | solution.py:29
Async XLA Ops:
  0.6 1.2 %copy-start = (bf16[1,2,4,16,3840]{4,3,2,1,0:T(8,128)(2,1)S(1)}, bf16[1,2,4,16,3840]{4,3,2,1,0:T(8,128)(2,1)}, u32[]{:S(2)}) copy-start(bf16[1,2,4,16,3840]{4,3,2,1,0:T(8,128)(2,1)} %param.10) | copy-start | bytes 2949124
  1.8 1.2 %copy-start.1 = (bf16[2,4,16,3840]{3,2,1,0:T(8,128)(2,1)S(1)}, bf16[2,4,16,3840]{3,2,1,0:T(8,128)(2,1)}, u32[]{:S(2)}) copy-start(bf16[2,4,16,3840]{3,2,1,0:T(8,128)(2,1)} %param.11) | copy-start | bytes 2949124
  76.3 1.5 %copy-start.2 = (f32[1,960,512]{2,1,0:T(8,128)S(1)}, f32[1,960,512]{2,1,0:T(8,128)}, u32[]{:S(2)}) copy-start(f32[1,960,512]{2,1,0:T(8,128)} %param.7) | copy-start | bytes 5898244
  76.3 1.8 %copy-start.3 = (bf16[1,960,512]{2,1,0:T(8,128)(2,1)S(1)}, bf16[1,960,512]{2,1,0:T(8,128)(2,1)}, u32[]{:S(2)}) copy-start(bf16[1,960,512]{2,1,0:T(8,128)(2,1)} %param.9) | copy-start | bytes 2949124
  76.3 2.1 %copy-start.4 = (bf16[1,960,512]{2,1,0:T(8,128)(2,1)S(1)}, bf16[1,960,512]{2,1,0:T(8,128)(2,1)}, u32[]{:S(2)}) copy-start(bf16[1,960,512]{2,1,0:T(8,128)(2,1)} %param.8) | copy-start | bytes 2949124

commit v5 on v4

--- a/solution.py
+++ b/solution.py
@@ -46,7 +46,6 @@
     chunk = features // chunks
     columns = [pl.ds(c * chunk, chunk) for c in range(chunks)]
     lower = sections // 2
-    late = lower + sections // 4
     partner = sections - 1 - position
     below = lax.rem(position + sections - 1, sections)
     above = lax.rem(position + 1, sections)
@@ -108,7 +107,7 @@
             ex_recv.at[kind, apart, k], {"dp": peer},
         )
 
-    @pl.when((position == 0) | ((position >= lower) & (position < late)))
+    @pl.when((position == 0) | (position >= lower))
     def _():
         swap_each(lambda copy: copy.start())
 
@@ -204,10 +203,6 @@
         advance(k)
         if k + 1 < pieces:
             prepare(k + 1)
-
-    @pl.when(position >= late)
-    def _():
-        swap_each(lambda copy: copy.start())
 
     @pl.when(position >= lower - 1)
     def _():

time: 82.7 us -> 77.6 us (0.938)
  Pallas kernels: 73.2 us -> 68.1 us
    pallas_call x1, Pallas kernels: 73.2 us -> 68.1 us  [shards(): pl.pallas_call(functools.partial(chain_kernel, n_dp, sections), out_shape...]
where the time goes in v5:
time: 77.6 us; the launch traced here: 77.4 us
  Pallas kernels  68.1 us (88%)
  other arithmetic  4.08 us (5%)
  local copies, waits for them, and re-layouts  3.53 us (5%)
  matrix products  0.92 us (1%)
    pallas_call x1, Pallas kernels, shards(): pl.pallas_call(functools.partial(chain_kernel, n_dp, sections), out_shape...  68.1 us
    convert_element_type x1, other arithmetic, adamw(): second_new.astype(jnp.bfloat16)  4.08 us
    unnamed x10, local copies, waits for them, and re-layouts  3.53 us

profile of v5, /device:TPU:0, one launch (start us, length us, event | category | flops | bytes accessed | tf_op | source)
XLA Modules:
  0.0 77.4 jit_solution(15424009417632887937)
XLA Ops:
  0.6 0.0 copy-start
  0.6 1.2 %copy-done = bf16[1,2,4,16,3840]{4,3,2,1,0:T(8,128)(2,1)S(1)} copy-done((bf16[1,2,4,16,3840]{4,3,2,1,0:T(8,128)(2,1)S(1)}, bf16[1,2,4,16,3840]{4,3,2,1,0:T(8,128)(2,1)}, u32[]{:S(2)}) %copy-start) | copy-done | bytes 983064
  1.8 0.0 copy-start.1
  1.8 1.2 %copy-done.1 = bf16[2,4,16,3840]{3,2,1,0:T(8,128)(2,1)S(1)} copy-done((bf16[2,4,16,3840]{3,2,1,0:T(8,128)(2,1)S(1)}, bf16[2,4,16,3840]{3,2,1,0:T(8,128)(2,1)}, u32[]{:S(2)}) %copy-start.1) | copy-done | bytes 983064
  3.0 68.1 %shard_map.85 = (bf16[4,8,16,960]{3,2,1,0:T(8,128)(2,1)S(1)}, bf16[4,8,16,960]{3,2,1,0:T(8,128)(2,1)S(1)}, bf16[4,8,16,512]{3,2,1,0:T(8,128)(2,1)S(1)}) custom-call(bf16[2,3840,512]{2,1,0:T(8,128)(2,1)} %bitcast.18, bf16[8,16,3840]{2,1,0:T(8,128)(2,1)S(1)} %bitcast.14, bf16[8,16,3840]{2,1,0:T(8,128)(2,1)S(1)} %bitcast.15), custom_call_target="tpu_custom_call" | custom-call | flops 754974720 | bytes 3932160 | tf_op jit(solution)/shard_map/pallas_call | solution.py:236
  71.2 0.0 copy-start.2
  71.2 0.0 copy-start.3
  71.2 0.0 copy-start.4
  71.2 0.5 convolution_bitcast_fusion
  71.7 0.5 convolution_bitcast_fusion.1
  72.2 0.6 copy-done.2
  72.7 0.2 copy-done.3
  73.0 0.3 copy-done.4
  73.3 4.1 %fusion.2 = (bf16[1,960,512]{2,1,0:T(8,128)(2,1)}, f32[1,960,512]{2,1,0:T(8,128)}, bf16[1,960,512]{2,1,0:T(8,128)(2,1)}) fusion(f32[1,960,256]{2,1,0:T(8,128)S(1)} %convolution_bitcast_fusion, f32[1,960,256]{2,1,0:T(8,128)S(1)} %convolution_bitcast_fusion.1, bf16[1,960,512]{2,1,0:T(8,128)(2,1)S(1)} %copy-done.3, f32[1,960,512]{2,1,0:T(8,128)S(1)} %copy-done.2, ...), kind=kLoop, calls=%fused_computation.8 | loop fusion | flops 9830400 | bytes 9830400 | tf_op jit(solution)/shard_map/convert_element_type | solution.py:29
Async XLA Ops:
  0.6 1.2 %copy-start = (bf16[1,2,4,16,3840]{4,3,2,1,0:T(8,128)(2,1)S(1)}, bf16[1,2,4,16,3840]{4,3,2,1,0:T(8,128)(2,1)}, u32[]{:S(2)}) copy-start(bf16[1,2,4,16,3840]{4,3,2,1,0:T(8,128)(2,1)} %param.10) | copy-start | bytes 2949124
  1.8 1.2 %copy-start.1 = (bf16[2,4,16,3840]{3,2,1,0:T(8,128)(2,1)S(1)}, bf16[2,4,16,3840]{3,2,1,0:T(8,128)(2,1)}, u32[]{:S(2)}) copy-start(bf16[2,4,16,3840]{3,2,1,0:T(8,128)(2,1)} %param.11) | copy-start | bytes 2949124
  71.2 1.5 %copy-start.2 = (f32[1,960,512]{2,1,0:T(8,128)S(1)}, f32[1,960,512]{2,1,0:T(8,128)}, u32[]{:S(2)}) copy-start(f32[1,960,512]{2,1,0:T(8,128)} %param.7) | copy-start | bytes 5898244
  71.2 1.8 %copy-start.3 = (bf16[1,960,512]{2,1,0:T(8,128)(2,1)S(1)}, bf16[1,960,512]{2,1,0:T(8,128)(2,1)}, u32[]{:S(2)}) copy-start(bf16[1,960,512]{2,1,0:T(8,128)(2,1)} %param.9) | copy-start | bytes 2949124
  71.2 2.1 %copy-start.4 = (bf16[1,960,512]{2,1,0:T(8,128)(2,1)S(1)}, bf16[1,960,512]{2,1,0:T(8,128)(2,1)}, u32[]{:S(2)}) copy-start(bf16[1,960,512]{2,1,0:T(8,128)(2,1)} %param.8) | copy-start | bytes 2949124

commit v6 on v5

--- a/solution.py
+++ b/solution.py
@@ -34,7 +34,6 @@
     normed_all, wide_all, narrow_all,
     w, here, arrived, outgoing, swapped, normed_cut, wide_cut, latents, scales,
     w_sem, here_sem, cot_sem, ex_send, ex_recv, chain_send, chain_recv, swap_send, swap_recv,
-    turn,
 ):
     me = lax.axis_index("dp")
     position = lax.axis_index("pipe")
@@ -45,7 +44,6 @@
     chunks = chain_send.shape[1]
     chunk = features // chunks
     columns = [pl.ds(c * chunk, chunk) for c in range(chunks)]
-    lower = sections // 2
     partner = sections - 1 - position
     below = lax.rem(position + sections - 1, sections)
     above = lax.rem(position + 1, sections)
@@ -107,9 +105,7 @@
             ex_recv.at[kind, apart, k], {"dp": peer},
         )
 
-    @pl.when((position == 0) | (position >= lower))
-    def _():
-        swap_each(lambda copy: copy.start())
+    swap_each(lambda copy: copy.start())
 
     here_copy.wait()
     w_copy.wait()
@@ -187,26 +183,12 @@
 
     prepare(0)
 
-    @pl.when((position > 0) & (position < lower))
-    def _():
-        pl.semaphore_wait(turn, 1)
-        swap_each(lambda copy: copy.start())
-
-    @pl.when(position < lower - 1)
-    def _():
-        swap_each(lambda copy: copy.wait_send())
-        pl.semaphore_signal(
-            turn, inc=1, device_id={"pipe": above}, device_id_type=pl.DeviceIdType.MESH
-        )
-
     for k in range(pieces):
         advance(k)
         if k + 1 < pieces:
             prepare(k + 1)
 
-    @pl.when(position >= lower - 1)
-    def _():
-        swap_each(lambda copy: copy.wait_send())
+    swap_each(lambda copy: copy.wait_send())
 
     @pl.when(position > 0)
     def _():
@@ -261,7 +243,6 @@
             pltpu.SemaphoreType.DMA((pieces, chunks)),
             pltpu.SemaphoreType.DMA((pieces // 2, chunks)),
             pltpu.SemaphoreType.DMA((pieces // 2, chunks)),
-            pltpu.SemaphoreType.REGULAR,
         ],
         compiler_params=pltpu.CompilerParams(
             collective_id=0, has_side_effects=True, vmem_limit_bytes=44 * 2**20

time: 77.6 us -> 77.5 us (level)
  no operation moved by 1% of the time
where the time goes in v6:
time: 77.5 us; the launch traced here: 77.3 us
  Pallas kernels  68.1 us (88%)
  other arithmetic  4.08 us (5%)
  local copies, waits for them, and re-layouts  3.53 us (5%)
  matrix products  0.92 us (1%)
    pallas_call x1, Pallas kernels, shards(): pl.pallas_call(functools.partial(chain_kernel, n_dp, sections), out_shape...  68.1 us
    convert_element_type x1, other arithmetic, adamw(): second_new.astype(jnp.bfloat16)  4.08 us
    unnamed x10, local copies, waits for them, and re-layouts  3.53 us

profile of v6, /device:TPU:0, one launch (start us, length us, event | category | flops | bytes accessed | tf_op | source)
XLA Modules:
  0.0 77.3 jit_solution(2743617426768633285)
XLA Ops:
  0.6 0.0 copy-start
  0.6 1.2 %copy-done = bf16[1,2,4,16,3840]{4,3,2,1,0:T(8,128)(2,1)S(1)} copy-done((bf16[1,2,4,16,3840]{4,3,2,1,0:T(8,128)(2,1)S(1)}, bf16[1,2,4,16,3840]{4,3,2,1,0:T(8,128)(2,1)}, u32[]{:S(2)}) %copy-start) | copy-done | bytes 983064
  1.8 0.0 copy-start.1
  1.8 1.2 %copy-done.1 = bf16[2,4,16,3840]{3,2,1,0:T(8,128)(2,1)S(1)} copy-done((bf16[2,4,16,3840]{3,2,1,0:T(8,128)(2,1)S(1)}, bf16[2,4,16,3840]{3,2,1,0:T(8,128)(2,1)}, u32[]{:S(2)}) %copy-start.1) | copy-done | bytes 983064
  3.0 68.1 %shard_map.85 = (bf16[4,8,16,960]{3,2,1,0:T(8,128)(2,1)S(1)}, bf16[4,8,16,960]{3,2,1,0:T(8,128)(2,1)S(1)}, bf16[4,8,16,512]{3,2,1,0:T(8,128)(2,1)S(1)}) custom-call(bf16[2,3840,512]{2,1,0:T(8,128)(2,1)} %bitcast.18, bf16[8,16,3840]{2,1,0:T(8,128)(2,1)S(1)} %bitcast.14, bf16[8,16,3840]{2,1,0:T(8,128)(2,1)S(1)} %bitcast.15), custom_call_target="tpu_custom_call" | custom-call | flops 754974720 | bytes 3932160 | tf_op jit(solution)/shard_map/pallas_call | solution.py:218
  71.2 0.0 copy-start.2
  71.2 0.0 copy-start.3
  71.2 0.0 copy-start.4
  71.2 0.5 convolution_bitcast_fusion
  71.7 0.5 convolution_bitcast_fusion.1
  72.1 0.6 copy-done.2
  72.7 0.2 copy-done.3
  73.0 0.3 copy-done.4
  73.3 4.1 %fusion.2 = (bf16[1,960,512]{2,1,0:T(8,128)(2,1)}, f32[1,960,512]{2,1,0:T(8,128)}, bf16[1,960,512]{2,1,0:T(8,128)(2,1)}) fusion(f32[1,960,256]{2,1,0:T(8,128)S(1)} %convolution_bitcast_fusion, f32[1,960,256]{2,1,0:T(8,128)S(1)} %convolution_bitcast_fusion.1, bf16[1,960,512]{2,1,0:T(8,128)(2,1)S(1)} %copy-done.3, f32[1,960,512]{2,1,0:T(8,128)S(1)} %copy-done.2, ...), kind=kLoop, calls=%fused_computation.8 | loop fusion | flops 9830400 | bytes 9830400 | tf_op jit(solution)/shard_map/convert_element_type | solution.py:29
Async XLA Ops:
  0.6 1.2 %copy-start = (bf16[1,2,4,16,3840]{4,3,2,1,0:T(8,128)(2,1)S(1)}, bf16[1,2,4,16,3840]{4,3,2,1,0:T(8,128)(2,1)}, u32[]{:S(2)}) copy-start(bf16[1,2,4,16,3840]{4,3,2,1,0:T(8,128)(2,1)} %param.10) | copy-start | bytes 2949124
  1.8 1.2 %copy-start.1 = (bf16[2,4,16,3840]{3,2,1,0:T(8,128)(2,1)S(1)}, bf16[2,4,16,3840]{3,2,1,0:T(8,128)(2,1)}, u32[]{:S(2)}) copy-start(bf16[2,4,16,3840]{3,2,1,0:T(8,128)(2,1)} %param.11) | copy-start | bytes 2949124
  71.2 1.5 %copy-start.2 = (f32[1,960,512]{2,1,0:T(8,128)S(1)}, f32[1,960,512]{2,1,0:T(8,128)}, u32[]{:S(2)}) copy-start(f32[1,960,512]{2,1,0:T(8,128)} %param.7) | copy-start | bytes 5898244
  71.2 1.8 %copy-start.3 = (bf16[1,960,512]{2,1,0:T(8,128)(2,1)S(1)}, bf16[1,960,512]{2,1,0:T(8,128)(2,1)}, u32[]{:S(2)}) copy-start(bf16[1,960,512]{2,1,0:T(8,128)(2,1)} %param.9) | copy-start | bytes 2949124
  71.2 2.1 %copy-start.4 = (bf16[1,960,512]{2,1,0:T(8,128)(2,1)S(1)}, bf16[1,960,512]{2,1,0:T(8,128)(2,1)}, u32[]{:S(2)}) copy-start(bf16[1,960,512]{2,1,0:T(8,128)(2,1)} %param.8) | copy-start | bytes 2949124
